TPU v7x, 768 devices: a whole 4x8x12 slice. The times are simulated.
768 devices in a mesh: rep: 48 (over z, x), fsdp: 16 (over y, core).
Axes of the slice: x: 4, y: 8, z: 12, core: 2. Of those that a mesh axis runs over, the one named last changes fastest.
Arguments:
- grad_parts: bfloat16 [48, 48, 512, 512], P('rep', None, 'fsdp'), may hold values from -0.09375 to 0.09375
- owner: int32 [48], P('rep'), may hold values from 0 to 15
- left_stat: bfloat16 [48, 16, 512, 512], P('rep', 'fsdp'), may hold values from -1 to 5, as said below
- right_stat: bfloat16 [48, 16, 512, 512], P('rep', 'fsdp'), may hold values from -1 to 5, as said below
- left_root: bfloat16 [48, 16, 512, 512], P('rep', 'fsdp'), may hold values from -1 to 4, as said below
- right_root: bfloat16 [48, 16, 512, 512], P('rep', 'fsdp'), may hold values from -1 to 4, as said below
Outputs:
- left_new: bfloat16 [48, 16, 512, 512], P('rep', 'fsdp')
- right_new: bfloat16 [48, 16, 512, 512], P('rep', 'fsdp')
- update: bfloat16 [48, 512, 512], P('rep', 'fsdp')
Inputs may be any that keep to these rules, and one draw needn't show every extreme that they name: `left_stat`: symmetric. `right_stat`: symmetric. `left_root`: symmetric. `right_root`: symmetric.
All inputs are finite; a program needn't handle non-finite values.
Results may differ from a plain program's by a relative error of at most 0.0057.
Values may be sent and summed in bfloat16 or wider, within the bound.
No kernel may reach another device: no remote copies, remote signals or barrier semaphores. Data moves between devices by JAX's collectives and lax.ppermute only.
A program may use at most 32 MiB of HBM per device.

v0:
```python
import jax
import jax.numpy as jnp
from jax import lax
from jax.sharding import PartitionSpec as P

epsilon = 1e-06


def spread(value, axis, source):
    kept = jnp.where(lax.axis_index(axis) == source, value, 0).astype(value.dtype)
    return lax.psum(kept, axis)


def gram_pair(gradient, left_slot, right_slot):
    rows_gram = lax.dot_general(
        gradient, gradient, (((1,), (1,)), ((), ())), preferred_element_type=jnp.float32
    )
    cols_gram = lax.dot_general(
        gradient, gradient, (((0,), (0,)), ((), ())), preferred_element_type=jnp.float32
    )
    left_out = (left_slot.astype(jnp.float32) + rows_gram).astype(jnp.bfloat16)
    right_out = (right_slot.astype(jnp.float32) + cols_gram).astype(jnp.bfloat16)
    return (left_out, right_out)


def precondition(left_rows, gradient, right_factor):
    middle = jnp.dot(left_rows, gradient, preferred_element_type=jnp.float32).astype(jnp.bfloat16)
    return jnp.dot(middle, right_factor, preferred_element_type=jnp.float32)


def on_device(grad_parts, owner, left_stat, right_stat, left_root, right_root):
    partial_value = grad_parts[0].astype(jnp.float32)
    summed = lax.psum_scatter(partial_value, "rep", scatter_dimension=0, tiled=True)
    rows_here = summed[0].astype(jnp.bfloat16)
    gradient = lax.all_gather(rows_here, "fsdp", axis=0, tiled=True)
    slab_rows = rows_here.shape[0]
    my_index = lax.axis_index("fsdp")
    holder = owner[0]
    is_owner = holder == my_index
    left_slot = left_stat[0, 0]
    right_slot = right_stat[0, 0]

    def updated(unused):
        return gram_pair(gradient, left_slot, right_slot)

    def unchanged(unused):
        return (left_slot, right_slot)

    left_out, right_out = lax.cond(is_owner, updated, unchanged, 0)

    def compute_update(unused):
        product = precondition(left_root[0, 0], gradient, right_root[0, 0])
        factor_norm = lax.rsqrt(jnp.mean(product * product) + epsilon)
        return (product * factor_norm).astype(jnp.bfloat16)

    def no_update(unused):
        return jnp.zeros(gradient.shape, jnp.bfloat16)

    own_update = lax.cond(is_owner, compute_update, no_update, 0)
    full_update = spread(own_update, "fsdp", holder)
    update = lax.dynamic_slice_in_dim(full_update, my_index * slab_rows, slab_rows, 0)
    return (left_out[None, None], right_out[None, None], update[None])


def solution(mesh):
    return jax.shard_map(
        on_device,
        mesh=mesh,
        in_specs=(
            P("rep", None, "fsdp", None),
            P("rep"),
            P("rep", "fsdp", None, None),
            P("rep", "fsdp", None, None),
            P("rep", "fsdp", None, None),
            P("rep", "fsdp", None, None),
        ),
        out_specs=(
            P("rep", "fsdp", None, None),
            P("rep", "fsdp", None, None),
            P("rep", "fsdp", None),
        ),
        check_vma=False,
    )
```

profile of v0, /device:TPU:1, one launch (start us, length us, event | category | flops | bytes accessed | tf_op | source)
XLA Modules:
  0.0 599.9 jit_solution(6973865195623295112)
XLA Ops:
  7.2 0.0 copy-start.2
  7.2 0.0 reduce-scatter.2.cloned.1.call-start
  7.2 1.4 copy-done.2
  8.6 2.1 bitcast_convert_fusion
  10.6 0.0 reduce-scatter.2.cloned.1.call-update
  10.7 0.0 all-reduce.2.cloned.1.call-start
  11.4 433.3 %reduce-scatter.2.cloned.1.call-done = f32[1,32,512]{2,1,0:T(8,128)} async-done(((f32[48,32,512]{2,1,0:T(8,128)}), f32[1,32,512]{2,1,0:T(8,128)}) %reduce-scatter.2.cloned.1.call-update) | async-done | bytes 65552 | tf_op jit(solution)/shard_map/reduce_scatter | solution.py:33
  444.6 0.8 convert_element_type.39
  445.5 27.1 %all-gather = bf16[1,512,512]{2,1,0:T(8,128)(2,1)S(1)} all-gather(bf16[1,32,512]{2,1,0:T(8,128)(2,1)S(1)} %convert_element_type.39), channel_id=2, replica_groups=mesh['rep'=48,'fsdp'=16] {'fsdp'}, dimensions={1}, use_global_device_ids=true | all-gather | bytes 557056 | tf_op jit(solution)/shard_map/all_gather | solution.py:35
  472.6 0.0 copy-start.1
  472.6 0.0 copy-start.4
  472.6 0.8 broadcast_select_fusion
  473.5 0.0 all-reduce.2.cloned.1.call-update
  473.5 0.2 copy-done.1
  473.7 0.2 copy-done.4
  474.0 0.0 copy-start
  474.0 0.0 copy-start.3
  474.0 117.7 %all-reduce.2.cloned.1.call-done = bf16[512,512]{1,0:T(8,128)(2,1)} async-done(((bf16[512,512]{1,0:T(8,128)(2,1)}), bf16[512,512]{1,0:T(8,128)(2,1)}) %all-reduce.2.cloned.1.call-update) | async-done | bytes 524304 | tf_op jit(solution)/shard_map/psum | solution.py:11
  591.7 1.4 dynamic-slice_bitcast_fusion
  593.1 0.0 copy-done
  593.1 0.0 copy-done.3
  (3 shorter events, 0.1 us)
Async XLA Ops:
  7.2 1.4 copy-start.2
  7.2 437.4 %reduce-scatter.2.cloned.1.call-start = ((), (), s32[]{:S(2)}) async-start(), calls=%async_computation.1 | async-start | bytes 3211264 | tf_op jit(solution)/shard_map/reduce_scatter | solution.py:33
  10.7 581.0 %all-reduce.2.cloned.1.call-start = ((), (), s32[]{:S(2)}) async-start(), calls=%async_computation.2 | async-start | bytes 1048576 | tf_op jit(solution)/shard_map/psum | solution.py:11
  472.6 1.2 copy-start.1
  472.6 1.4 copy-start.4
  474.0 119.1 %copy-start = (bf16[1,1,512,512]{3,2,1,0:T(8,128)(2,1)}, bf16[1,1,512,512]{3,2,1,0:T(8,128)(2,1)S(1)}, u32[]{:S(2)}) copy-start(bf16[1,1,512,512]{3,2,1,0:T(8,128)(2,1)S(1)} %get-tuple-element.39) | copy-start | bytes 1572868
  474.0 119.1 %copy-start.3 = (bf16[1,1,512,512]{3,2,1,0:T(8,128)(2,1)}, bf16[1,1,512,512]{3,2,1,0:T(8,128)(2,1)S(1)}, u32[]{:S(2)}) copy-start(bf16[1,1,512,512]{3,2,1,0:T(8,128)(2,1)S(1)} %get-tuple-element.40) | copy-start | bytes 1572868
Sparse Core Ops, SparseCore 0:
  13.0 431.5 reduce-scatter.1
  473.6 118.0 all-reduce.1
where the time goes:
time: 600 us
  waiting for transfers between devices  551 us (92%)
  blocking collectives  27.1 us (5%)
  between operations  14.7 us (2%)
    reduce_scatter x1, waiting for transfers between devices, on_device(): lax.psum_scatter(partial_value, 'rep', scatter_dimension=0, tiled=True)  433 us
    psum x1, waiting for transfers between devices, spread(): return lax.psum(kept, axis)  118 us
    all_gather x1, blocking collectives, on_device(): gradient = lax.all_gather(rows_here, 'fsdp', axis=0, tiled=True)  27.1 us
  transfers between devices with their start and end apart: 2, of which 2 were waited for; matrix products, arithmetic and copies ran while one was open for 0% of the time, Pallas kernels for 0%

commit v1 on v0

v1 whole, which is shorter than its diff:
```python
import jax
import jax.numpy as jnp
from jax import lax
from jax.sharding import Mesh, PartitionSpec as P

epsilon = 1e-06
AXES = ("zh", "zl", "x", "y", "core")
SIZES = (6, 2, 4, 8, 2)
REP = ("zh", "zl", "x")
FSDP = ("y", "core")


def rotate(value, axis, size, step):
    return lax.ppermute(value, axis, [(i, (i + step) % size) for i in range(size)])


def after(values, event):
    return lax.optimization_barrier((values, event))[0]


def pack(left, right):
    row = lax.broadcasted_iota(jnp.int32, left.shape, 0)
    col = lax.broadcasted_iota(jnp.int32, left.shape, 1)
    both = jnp.where(row <= col, left, right)
    diagonal = jnp.sum(jnp.where(row == col, right, 0).astype(jnp.float32), axis=0)
    diagonal = jnp.broadcast_to(diagonal.astype(jnp.bfloat16)[None], (8, 512))
    upper = jnp.concatenate([both[:256], diagonal], axis=0)
    lower = jnp.concatenate([both[256:], diagonal], axis=0)
    return upper, lower


def unpack(upper, lower):
    both = jnp.concatenate([upper[:256], lower[:256]], axis=0)
    flipped = both.T
    row = lax.broadcasted_iota(jnp.int32, both.shape, 0)
    col = lax.broadcasted_iota(jnp.int32, both.shape, 1)
    left = jnp.where(row <= col, both, flipped)
    right = jnp.where(row == col, upper[256][None], jnp.where(row > col, both, flipped))
    return left, right


def on_device(grad_parts, owner, left_stat, right_stat, left_root, right_root):
    holder = owner[0]
    my_index = lax.axis_index(FSDP)
    y = lax.axis_index("y")
    first = lax.axis_index("core") == 0
    away = lax.rem(y - holder // 2 + 8, 8)
    upper, lower = pack(left_root[0, 0], right_root[0, 0])
    keep = jnp.where(first, upper, lower)
    got = rotate(jnp.where(first, lower, upper), "core", 2, 1)
    here = jnp.where(holder == my_index, keep, got)
    up = rotate(here, "y", 8, 3)
    down = rotate(here, "y", 8, -3)

    parts = grad_parts[0].reshape(6, 8, 32, 512)
    parts = lax.all_to_all(parts, ("zl", "x"), 1, 1, tiled=True)
    parts = jnp.sum(parts.astype(jnp.float32), axis=1).astype(jnp.bfloat16)
    up, down = after((up, down), parts)
    here = jnp.where(away == 0, here, jnp.where(away == 3, up, down))
    up = rotate(here, "y", 8, 1)
    down = rotate(here, "y", 8, -1)
    parts = lax.all_to_all(parts, "zh", 0, 0, tiled=True)
    rows = jnp.sum(parts.astype(jnp.float32), axis=0).astype(jnp.bfloat16)
    gradient = lax.all_gather(rows, FSDP, axis=0, tiled=True)
    up, down = after((up, down), parts)
    here = jnp.where((away == 0) | (away == 3) | (away == 5), here, jnp.where((away == 1) | (away == 4) | (away == 6), up, down))
    other = rotate(here, "core", 2, 1)
    left, right = unpack(jnp.where(first, here, other), jnp.where(first, other, here))

    middle = jnp.dot(left, gradient, preferred_element_type=jnp.float32).astype(jnp.bfloat16)
    product = jnp.dot(middle, right, preferred_element_type=jnp.float32)
    scale = lax.rsqrt(jnp.mean(product * product) + epsilon)
    update = lax.dynamic_slice_in_dim(product, my_index * 32, 32, 0)
    update = (update * scale).astype(jnp.bfloat16)

    owned = holder == my_index
    rows_gram = lax.dot_general(
        gradient, gradient, (((1,), (1,)), ((), ())), preferred_element_type=jnp.float32
    )
    cols_gram = lax.dot_general(
        gradient, gradient, (((0,), (0,)), ((), ())), preferred_element_type=jnp.float32
    )
    left_slot = left_stat[0, 0]
    right_slot = right_stat[0, 0]
    left_out = (left_slot.astype(jnp.float32) + jnp.where(owned, rows_gram, 0.0)).astype(jnp.bfloat16)
    right_out = (right_slot.astype(jnp.float32) + jnp.where(owned, cols_gram, 0.0)).astype(jnp.bfloat16)
    return (left_out[None, None], right_out[None, None], update[None])


def solution(mesh):
    grid = Mesh(mesh.devices.reshape(SIZES), AXES)
    slots = P(REP, FSDP, None, None)
    return jax.shard_map(
        on_device,
        mesh=grid,
        in_specs=(P(REP, None, FSDP, None), P(REP), slots, slots, slots, slots),
        out_specs=(slots, slots, P(REP, FSDP, None)),
        check_vma=False,
    )
```

time: 600 us -> 86.9 us (0.14)
  waiting for transfers between devices: 551 us -> 3.09 us
  starting transfers between devices: 0.08 us -> 49 us
  between operations: 14.7 us -> 2.15 us
    reduce_scatter x1 -> x0, waiting for transfers between devices: 433 us -> none  [on_device(): lax.psum_scatter(partial_value, 'rep', scatter_dimension=0, tiled=True)]
    psum x1 -> x0, waiting for transfers between devices: 118 us -> none  [spread(): return lax.psum(kept, axis)]
    ppermute x0 -> x6, starting transfers between devices: none -> 27 us  [rotate(): lax.ppermute(value, axis, [(i, (i + step) % size) for i in range(size)])]
    all_to_all x0 -> x2, starting transfers between devices: none -> 22 us  [the longest x1 15.3 us: on_device(): parts = lax.all_to_all(parts, 'zh', 0, 0, tiled=True)]
  transfers between devices with their start and end apart: 2 -> 8, of which waited for: 2 -> 2; matrix products, arithmetic and copies ran while one was open for 0% -> 4% of each run, Pallas kernels for 0% -> 0%
where the time goes in v1:
time: 86.9 us; the launch traced here: 86.4 us
  starting transfers between devices  49 us (56%)
  blocking collectives  22.9 us (26%)
  matrix products  3.99 us (5%)
  waiting for transfers between devices  3.09 us (4%)
  local copies, waits for them, and re-layouts  3.07 us (4%)
  between operations  2.15 us (2%)
  other arithmetic  2.11 us (2%)
    ppermute x6, starting transfers between devices, rotate(): lax.ppermute(value, axis, [(i, (i + step) % size) for i in range(size)])  27 us
    all_gather x1, blocking collectives, on_device(): gradient = lax.all_gather(rows, FSDP, axis=0, tiled=True)  22.9 us
    all_to_all x1, starting transfers between devices, on_device(): parts = lax.all_to_all(parts, 'zh', 0, 0, tiled=True)  15.3 us
    all_to_all x1, starting transfers between devices, on_device(): parts = lax.all_to_all(parts, ('zl', 'x'), 1, 1, tiled=True)  6.79 us
    another operation x1, local copies, waits for them, and re-layouts, on_device(): parts = grad_parts[0].reshape(6, 8, 32, 512)  2.76 us
    all_to_all x1, waiting for transfers between devices, on_device(): parts = lax.all_to_all(parts, 'zh', 0, 0, tiled=True)  2.58 us
  transfers between devices with their start and end apart: 8, of which 2 were waited for; matrix products, arithmetic and copies ran while one was open for 4% of the time, Pallas kernels for 0%

profile of v1, /device:TPU:1, one launch (start us, length us, event | category | flops | bytes accessed | tf_op | source)
XLA Modules:
  0.0 86.4 jit_solution(10937542265903828687)
XLA Ops:
  0.6 2.8 %copy.13 = bf16[6,8,32,512]{3,2,0,1:T(8,128)(2,1)} copy(bf16[6,8,32,512]{3,2,1,0:T(8,128)(2,1)} %bitcast.41) | data formatting | bytes 3145728 | tf_op jit(solution)/shard_map/reshape;squeeze | solution.py:55
  3.4 6.8 %all-to-all-start = ((bf16[6,8,32,512]{3,2,0,1:T(8,128)(2,1)}), bf16[6,8,32,512]{3,2,0,1:T(8,128)(2,1)S(1)}, u32[]{:S(2)}, u32[]{:S(2)}) async-start(bf16[6,8,32,512]{3,2,0,1:T(8,128)(2,1)} %copy.13), calls=%async_computation | async-start | bytes 3145728 | tf_op jit(solution)/shard_map/all_to_all | solution.py:56
  10.2 0.0 copy-done
  10.2 0.0 copy-done.1
  10.2 0.1 fusion.10
  10.4 0.1 broadcast_select_fusion.1
  10.4 9.4 %collective-permute-start = (bf16[264,512]{1,0:T(8,128)(2,1)S(1)}, bf16[264,512]{1,0:T(8,128)(2,1)S(1)}, u32[]{:S(2)}, u32[]{:S(2)}) collective-permute-start(bf16[264,512]{1,0:T(8,128)(2,1)S(1)} %broadcast_select_fusion.1), channel_id=1, source_target_pairs={{0,1},{1,0},{2,3},{3,2},{4,5},{5,4},{6,7},{7,6},{8,9},{9,8},{10,11... | collective-permute-start | bytes 811016 | tf_op jit(solution)/shard_map/ppermute | solution.py:14
  20.5 0.5 collective-permute-done
  21.0 0.1 select_select_fusion.2
  21.1 1.9 %collective-permute-start.1 = (bf16[264,512]{1,0:T(8,128)(2,1)S(1)}, bf16[264,512]{1,0:T(8,128)(2,1)S(1)}, u32[]{:S(2)}, u32[]{:S(2)}) collective-permute-start(bf16[264,512]{1,0:T(8,128)(2,1)S(1)} %select_select_fusion.2), channel_id=1, source_target_pairs={{0,6},{2,8},{4,10},{6,12},{8,14},{10,0},{12,2},{14,4},{1,7},{3,9},... | collective-permute-start | bytes 811016 | tf_op jit(solution)/shard_map/ppermute | solution.py:14
  23.0 6.4 %collective-permute-start.2 = (bf16[264,512]{1,0:T(8,128)(2,1)S(1)}, bf16[264,512]{1,0:T(8,128)(2,1)S(1)}, u32[]{:S(2)}, u32[]{:S(2)}) collective-permute-start(bf16[264,512]{1,0:T(8,128)(2,1)S(1)} %select_select_fusion.2), channel_id=1, source_target_pairs={{0,10},{2,12},{4,14},{6,0},{8,2},{10,4},{12,6},{14,8},{1,11},{3,13... | collective-permute-start | bytes 811016 | tf_op jit(solution)/shard_map/ppermute | solution.py:14
  29.4 0.0 all-to-all-done
  29.4 1.0 %reduce_sum.45 = bf16[6,32,512]{2,1,0:T(8,128)(2,1)} reduce(bf16[6,8,32,512]{3,2,0,1:T(8,128)(2,1)S(1)} %all-to-all-done, bf16[]{:T(256)} %constant.39.clone.1), dimensions={1}, to_apply=%region_0.1 | reduce | flops 688128 | bytes 1769474 | tf_op jit(solution)/shard_map/reduce_sum | solution.py:57
  30.3 15.3 %all-to-all-start.1 = ((bf16[6,32,512]{2,1,0:T(8,128)(2,1)}), bf16[6,32,512]{2,1,0:T(8,128)(2,1)S(1)}, u32[]{:S(2)}, u32[]{:S(2)}) async-start(bf16[6,32,512]{2,1,0:T(8,128)(2,1)} %reduce_sum.45), calls=%async_computation.1 | async-start | bytes 393216 | tf_op jit(solution)/shard_map/all_to_all | solution.py:62
  45.6 0.0 collective-permute-done.1
  45.6 0.0 collective-permute-done.2
  45.7 3.3 %collective-permute-start.3 = (bf16[264,512]{1,0:T(8,128)(2,1)S(1)}, bf16[264,512]{1,0:T(8,128)(2,1)S(1)}, u32[]{:S(2)}, u32[]{:S(2)}) collective-permute-start(bf16[264,512]{1,0:T(8,128)(2,1)S(1)} %select_select_fusion.1), channel_id=1, source_target_pairs={{0,2},{2,4},{4,6},{6,8},{8,10},{10,12},{12,14},{14,0},{1,3},{3,5},... | collective-permute-start | bytes 811016 | tf_op jit(solution)/shard_map/ppermute | solution.py:14
  49.0 3.8 %collective-permute-start.4 = (bf16[264,512]{1,0:T(8,128)(2,1)S(1)}, bf16[264,512]{1,0:T(8,128)(2,1)S(1)}, u32[]{:S(2)}, u32[]{:S(2)}) collective-permute-start(bf16[264,512]{1,0:T(8,128)(2,1)S(1)} %select_select_fusion.1), channel_id=1, source_target_pairs={{0,14},{2,0},{4,2},{6,4},{8,6},{10,8},{12,10},{14,12},{1,15},{3,1}... | collective-permute-start | bytes 811016 | tf_op jit(solution)/shard_map/ppermute | solution.py:14
  52.8 2.6 %all-to-all-done.1 = bf16[6,32,512]{2,1,0:T(8,128)(2,1)S(1)} async-done(((bf16[6,32,512]{2,1,0:T(8,128)(2,1)}), bf16[6,32,512]{2,1,0:T(8,128)(2,1)S(1)}, u32[]{:S(2)}, u32[]{:S(2)}) %all-to-all-start.1) | async-done | bytes 196640 | tf_op jit(solution)/shard_map/all_to_all | solution.py:62
  55.5 22.9 %all_gather.3 = bf16[512,512]{1,0:T(8,128)(2,1)S(1)} all-gather(bf16[32,512]{1,0:T(8,128)(2,1)S(1)} %reduce_sum.46), channel_id=1, replica_groups=mesh['zh'=6,'zl'=2,'x'=4,'y'=8,'core'=2] {'y','core'}, dimensions={0}, use_global_device_ids=true | all-gather | bytes 557056 | tf_op jit(solution)/shard_map/all_gather | solution.py:64
  78.4 0.0 collective-permute-done.3
  78.4 0.0 collective-permute-done.4
  78.4 0.1 select_select_fusion
  78.5 2.2 %collective-permute-start.5 = (bf16[264,512]{1,0:T(8,128)(2,1)S(1)}, bf16[264,512]{1,0:T(8,128)(2,1)S(1)}, u32[]{:S(2)}, u32[]{:S(2)}) collective-permute-start(bf16[264,512]{1,0:T(8,128)(2,1)S(1)} %select_select_fusion), channel_id=1, source_target_pairs={{0,1},{1,0},{2,3},{3,2},{4,5},{5,4},{6,7},{7,6},{8,9},{9,8},{10,11... | collective-permute-start | bytes 811016 | tf_op jit(solution)/shard_map/ppermute | solution.py:14
  80.7 0.0 copy-done.2
  80.7 1.3 %fusion.5 = bf16[1,1,512,512]{3,2,1,0:T(8,128)(2,1)} fusion(bf16[512,512]{1,0:T(8,128)(2,1)S(1)} %all_gather.3, bf16[1,1,512,512]{3,2,1,0:T(8,128)(2,1)S(1)} %copy-done.2, pred[]{:T(512)S(6)} %eq.33), kind=kOutput, calls=%fused_computation.8 | convolution fusion | flops 269484032 | bytes 1572865 | tf_op jit(solution)/shard_map/dot_general | solution.py:77
  82.0 0.0 copy-done.3
  82.0 1.3 %fusion.6 = bf16[1,1,512,512]{3,2,1,0:T(8,128)(2,1)} fusion(bf16[512,512]{1,0:T(8,128)(2,1)S(1)} %all_gather.3, bf16[1,1,512,512]{3,2,1,0:T(8,128)(2,1)S(1)} %copy-done.3, pred[]{:T(512)S(6)} %eq.33), kind=kOutput, calls=%fused_computation.9 | convolution fusion | flops 269484032 | bytes 1572865 | tf_op jit(solution)/shard_map/dot_general | solution.py:80
  83.2 0.0 collective-permute-done.5
  83.4 0.2 copy.14
  83.6 1.5 %multiply_reduce_fusion = (f32[]{:T(128)}, f32[512,512]{1,0:T(8,128)S(1)}) fusion(bf16[512,512]{0,1:T(8,128)(2,1)S(1)} %copy.14, bf16[512]{0:T(512)(128)(2,1)S(1)} %slice_reduce_fusion, bf16[256,512]{1,0:T(8,128)(2,1)S(1)} %slice_select_fusion, bf16[256,512]{1,0:T(8,128)(2,1)S(1)} %slice.22, bf16[512,512]{1,0:T(8,128)(2,1)S(1)} %all_gather.3), kind=kOutput, calls=%fused_computation.10 | convolution fusion | flops 541327360 | bytes 2622468 | tf_op jit(solution)/shard_map/dot_general | solution.py:71
  85.8 0.6 fusion.19
  (13 shorter events, 0.3 us)
Async XLA Ops:
  3.4 6.8 %copy-start = (bf16[1,1,512,512]{3,2,1,0:T(8,128)(2,1)S(1)}, bf16[1,1,512,512]{3,2,1,0:T(8,128)(2,1)}, u32[]{:S(2)}) copy-start(bf16[1,1,512,512]{3,2,1,0:T(8,128)(2,1)} %param.11) | copy-start | bytes 1572868
  3.4 6.8 %copy-start.1 = (bf16[1,1,512,512]{3,2,1,0:T(8,128)(2,1)S(1)}, bf16[1,1,512,512]{3,2,1,0:T(8,128)(2,1)}, u32[]{:S(2)}) copy-start(bf16[1,1,512,512]{3,2,1,0:T(8,128)(2,1)} %param.10) | copy-start | bytes 1572868
  3.4 26.0 %all-to-all-start = ((bf16[6,8,32,512]{3,2,0,1:T(8,128)(2,1)}), bf16[6,8,32,512]{3,2,0,1:T(8,128)(2,1)S(1)}, u32[]{:S(2)}, u32[]{:S(2)}) async-start(bf16[6,8,32,512]{3,2,0,1:T(8,128)(2,1)} %copy.13), calls=%async_computation | async-start | bytes 3145728 | tf_op jit(solution)/shard_map/all_to_all | solution.py:56
  10.4 10.5 %collective-permute-start = (bf16[264,512]{1,0:T(8,128)(2,1)S(1)}, bf16[264,512]{1,0:T(8,128)(2,1)S(1)}, u32[]{:S(2)}, u32[]{:S(2)}) collective-permute-start(bf16[264,512]{1,0:T(8,128)(2,1)S(1)} %broadcast_select_fusion.1), channel_id=1, source_target_pairs={{0,1},{1,0},{2,3},{3,2},{4,5},{5,4},{6,7},{7,6},{8,9},{9,8},{10,11... | collective-permute-start | bytes 811016 | tf_op jit(solution)/shard_map/ppermute | solution.py:14
  21.1 24.5 %collective-permute-start.1 = (bf16[264,512]{1,0:T(8,128)(2,1)S(1)}, bf16[264,512]{1,0:T(8,128)(2,1)S(1)}, u32[]{:S(2)}, u32[]{:S(2)}) collective-permute-start(bf16[264,512]{1,0:T(8,128)(2,1)S(1)} %select_select_fusion.2), channel_id=1, source_target_pairs={{0,6},{2,8},{4,10},{6,12},{8,14},{10,0},{12,2},{14,4},{1,7},{3,9},... | collective-permute-start | bytes 811016 | tf_op jit(solution)/shard_map/ppermute | solution.py:14
  23.0 22.6 %collective-permute-start.2 = (bf16[264,512]{1,0:T(8,128)(2,1)S(1)}, bf16[264,512]{1,0:T(8,128)(2,1)S(1)}, u32[]{:S(2)}, u32[]{:S(2)}) collective-permute-start(bf16[264,512]{1,0:T(8,128)(2,1)S(1)} %select_select_fusion.2), channel_id=1, source_target_pairs={{0,10},{2,12},{4,14},{6,0},{8,2},{10,4},{12,6},{14,8},{1,11},{3,13... | collective-permute-start | bytes 811016 | tf_op jit(solution)/shard_map/ppermute | solution.py:14
  30.3 25.1 %all-to-all-start.1 = ((bf16[6,32,512]{2,1,0:T(8,128)(2,1)}), bf16[6,32,512]{2,1,0:T(8,128)(2,1)S(1)}, u32[]{:S(2)}, u32[]{:S(2)}) async-start(bf16[6,32,512]{2,1,0:T(8,128)(2,1)} %reduce_sum.45), calls=%async_computation.1 | async-start | bytes 393216 | tf_op jit(solution)/shard_map/all_to_all | solution.py:62
  45.6 35.1 %copy-start.2 = (bf16[1,1,512,512]{3,2,1,0:T(8,128)(2,1)S(1)}, bf16[1,1,512,512]{3,2,1,0:T(8,128)(2,1)}, u32[]{:S(2)}) copy-start(bf16[1,1,512,512]{3,2,1,0:T(8,128)(2,1)} %param.8) | copy-start | bytes 1572868
  45.7 32.8 %collective-permute-start.3 = (bf16[264,512]{1,0:T(8,128)(2,1)S(1)}, bf16[264,512]{1,0:T(8,128)(2,1)S(1)}, u32[]{:S(2)}, u32[]{:S(2)}) collective-permute-start(bf16[264,512]{1,0:T(8,128)(2,1)S(1)} %select_select_fusion.1), channel_id=1, source_target_pairs={{0,2},{2,4},{4,6},{6,8},{8,10},{10,12},{12,14},{14,0},{1,3},{3,5},... | collective-permute-start | bytes 811016 | tf_op jit(solution)/shard_map/ppermute | solution.py:14
  49.0 29.4 %collective-permute-start.4 = (bf16[264,512]{1,0:T(8,128)(2,1)S(1)}, bf16[264,512]{1,0:T(8,128)(2,1)S(1)}, u32[]{:S(2)}, u32[]{:S(2)}) collective-permute-start(bf16[264,512]{1,0:T(8,128)(2,1)S(1)} %select_select_fusion.1), channel_id=1, source_target_pairs={{0,14},{2,0},{4,2},{6,4},{8,6},{10,8},{12,10},{14,12},{1,15},{3,1}... | collective-permute-start | bytes 811016 | tf_op jit(solution)/shard_map/ppermute | solution.py:14
  78.4 3.6 %copy-start.3 = (bf16[1,1,512,512]{3,2,1,0:T(8,128)(2,1)S(1)}, bf16[1,1,512,512]{3,2,1,0:T(8,128)(2,1)}, u32[]{:S(2)}) copy-start(bf16[1,1,512,512]{3,2,1,0:T(8,128)(2,1)} %param.9) | copy-start | bytes 1572868
  78.5 4.8 %collective-permute-start.5 = (bf16[264,512]{1,0:T(8,128)(2,1)S(1)}, bf16[264,512]{1,0:T(8,128)(2,1)S(1)}, u32[]{:S(2)}, u32[]{:S(2)}) collective-permute-start(bf16[264,512]{1,0:T(8,128)(2,1)S(1)} %select_select_fusion), channel_id=1, source_target_pairs={{0,1},{1,0},{2,3},{3,2},{4,5},{5,4},{6,7},{7,6},{8,9},{9,8},{10,11... | collective-permute-start | bytes 811016 | tf_op jit(solution)/shard_map/ppermute | solution.py:14

commit v2 on v1

v2 whole, which is shorter than its diff:
```python
import jax
import jax.numpy as jnp
from jax import lax
from jax.experimental import pallas as pl
from jax.experimental.pallas import tpu as pltpu
from jax.sharding import Mesh, PartitionSpec as P

epsilon = 1e-06
AXES = ("zh", "zl", "x", "y", "core")
SIZES = (6, 2, 4, 8, 2)
REP = ("zh", "zl", "x")
FSDP = ("y", "core")


def rotate(value, axis, size, step):
    return lax.ppermute(value, axis, [(i, (i + step) % size) for i in range(size)])


def after(values, event):
    return lax.optimization_barrier((values, event))[0]


def pack(left, right):
    row = lax.broadcasted_iota(jnp.int32, left.shape, 0)
    col = lax.broadcasted_iota(jnp.int32, left.shape, 1)
    both = jnp.where(row <= col, left, right)
    diagonal = jnp.sum(jnp.where(row == col, right, 0).astype(jnp.float32), axis=0)
    diagonal = jnp.broadcast_to(diagonal.astype(jnp.bfloat16)[None], (16, 512))
    upper = jnp.concatenate([both[:256], diagonal], axis=0)
    lower = jnp.concatenate([both[256:], diagonal], axis=0)
    return upper, lower


def regroup_kernel(source, target, held, sems):
    into = [
        pltpu.make_async_copy(source.at[:, to], held.at[to], sems.at[0, to]) for to in range(8)
    ]
    out = [pltpu.make_async_copy(held.at[to], target.at[to], sems.at[1, to]) for to in range(8)]
    for copy in into:
        copy.start()
    for to in range(8):
        into[to].wait()
        out[to].start()
    for copy in out:
        copy.wait()


def regroup(parts):
    anywhere = pl.BlockSpec(memory_space=pl.ANY)
    return pl.pallas_call(
        regroup_kernel,
        out_shape=jax.ShapeDtypeStruct((8, 6, 32, 512), jnp.bfloat16),
        in_specs=[anywhere],
        out_specs=anywhere,
        scratch_shapes=[
            pltpu.VMEM((8, 6, 32, 512), jnp.bfloat16),
            pltpu.SemaphoreType.DMA((2, 8)),
        ],
        compiler_params=pltpu.CompilerParams(vmem_limit_bytes=62 * 1024 * 1024),
    )(parts)


def finish_kernel(place, half, other, left_stat, right_stat, left_new, right_new, update,
                  gradient, roots, left_slot, right_slot, product, sems):
    into = [
        pltpu.make_async_copy(left_stat, left_slot, sems.at[0]),
        pltpu.make_async_copy(right_stat, right_slot, sems.at[1]),
    ]
    out = [
        pltpu.make_async_copy(left_slot, left_new, sems.at[2]),
        pltpu.make_async_copy(right_slot, right_new, sems.at[3]),
    ]
    for copy in into:
        copy.start()
    for source, core in ((half, place[2]), (other, 1 - place[2])):
        for y in range(8):
            at = pl.multiple_of((2 * y + core) * 32, 32)
            gradient[pl.ds(at, 32), :] = source[y * 32 : y * 32 + 32, :]
        roots[pl.ds(pl.multiple_of(core * 256, 256), 256), :] = source[256:512, :]
    value = gradient[...]
    owned = place[0] == 1
    for slot, side, arrive, leave in ((left_slot, 1, into[0], out[0]), (right_slot, 0, into[1], out[1])):
        gram = lax.dot_general(
            value, value, (((side,), (side,)), ((), ())), preferred_element_type=jnp.float32
        )
        arrive.wait()

        @pl.when(owned)
        def add():
            slot[...] = (slot[...].astype(jnp.float32) + gram).astype(jnp.bfloat16)

        leave.start()
    both = roots[...]
    diagonal = half[512:528, :].astype(jnp.float32)[0:1, :]
    flipped = both.T.astype(jnp.float32)
    both = both.astype(jnp.float32)
    row = lax.broadcasted_iota(jnp.int32, both.shape, 0)
    col = lax.broadcasted_iota(jnp.int32, both.shape, 1)
    left = jnp.where(row <= col, both, flipped).astype(jnp.bfloat16)
    right = jnp.where(row > col, both, jnp.where(row < col, flipped, diagonal)).astype(jnp.bfloat16)
    middle = jnp.dot(left, value, preferred_element_type=jnp.float32).astype(jnp.bfloat16)
    product[...] = jnp.dot(middle, right, preferred_element_type=jnp.float32)
    total = product[...]
    scale = lax.rsqrt(jnp.sum(total * total, keepdims=True) / (512.0 * 512.0) + epsilon)
    at = pl.multiple_of(place[1] * 32, 32)
    update[...] = (product[pl.ds(at, 32), :] * scale).astype(jnp.bfloat16)
    for copy in out:
        copy.wait()


def finish(place, half, other, left_stat, right_stat):
    square = jax.ShapeDtypeStruct((512, 512), jnp.bfloat16)
    anywhere = pl.BlockSpec(memory_space=pl.ANY)
    vmem = pl.BlockSpec(memory_space=pltpu.VMEM)
    return pl.pallas_call(
        finish_kernel,
        out_shape=(square, square, jax.ShapeDtypeStruct((32, 512), jnp.bfloat16)),
        in_specs=[pl.BlockSpec(memory_space=pltpu.SMEM), vmem, vmem, anywhere, anywhere],
        out_specs=(anywhere, anywhere, vmem),
        scratch_shapes=[
            pltpu.VMEM((512, 512), jnp.bfloat16),
            pltpu.VMEM((512, 512), jnp.bfloat16),
            pltpu.VMEM((512, 512), jnp.bfloat16),
            pltpu.VMEM((512, 512), jnp.bfloat16),
            pltpu.VMEM((512, 512), jnp.float32),
            pltpu.SemaphoreType.DMA((4,)),
        ],
        compiler_params=pltpu.CompilerParams(vmem_limit_bytes=24 * 1024 * 1024),
        cost_estimate=pl.CostEstimate(flops=8 * 512**3, bytes_accessed=4 * 512 * 1024, transcendentals=0),
    )(place, half, other, left_stat, right_stat)


def on_device(grad_parts, owner, left_stat, right_stat, left_root, right_root):
    holder = owner[0]
    my_index = lax.axis_index(FSDP)
    y = lax.axis_index("y")
    first = lax.axis_index("core") == 0
    away = lax.rem(y - holder // 2 + 8, 8)
    place = jnp.stack([(holder == my_index).astype(jnp.int32), my_index, lax.axis_index("core")])

    upper, lower = pack(left_root[0, 0], right_root[0, 0])
    keep = jnp.where(first, upper, lower)
    got = rotate(jnp.where(first, lower, upper), "core", 2, 1)
    here = jnp.where(holder == my_index, keep, got)
    up = rotate(here, "y", 8, 3)
    down = rotate(here, "y", 8, -3)

    parts = regroup(grad_parts[0].reshape(6, 8, 32, 512))
    parts = lax.all_to_all(parts, ("zl", "x"), 0, 0, tiled=True)
    parts = jnp.sum(parts.astype(jnp.float32), axis=0).astype(jnp.bfloat16)
    up, down = after((up, down), parts)
    here = jnp.where(away == 0, here, jnp.where(away == 3, up, down))
    up = rotate(here, "y", 8, 1)
    down = rotate(here, "y", 8, -1)
    parts = lax.all_to_all(parts, "zh", 0, 0, tiled=True)
    rows = jnp.sum(parts.astype(jnp.float32), axis=0).astype(jnp.bfloat16)

    spread = lax.all_to_all(jnp.broadcast_to(rows[None], (8, 32, 512)), "y", 0, 0, tiled=True)
    kept = (away == 0) | (away == 3) | (away == 5)
    here = jnp.where(kept, here, jnp.where((away == 1) | (away == 4) | (away == 6), up, down))
    half = jnp.concatenate([spread.reshape(256, 512), here], axis=0)
    other = rotate(half, "core", 2, 1)
    left_out, right_out, update = finish(place, half, other, left_stat[0, 0], right_stat[0, 0])
    return (left_out[None, None], right_out[None, None], update[None])


def solution(mesh):
    grid = Mesh(mesh.devices.reshape(SIZES), AXES)
    slots = P(REP, FSDP, None, None)
    return jax.shard_map(
        on_device,
        mesh=grid,
        in_specs=(P(REP, None, FSDP, None), P(REP), slots, slots, slots, slots),
        out_specs=(slots, slots, P(REP, FSDP, None)),
        check_vma=False,
    )
```

time: 86.9 us -> 84.9 us (0.977)
  blocking collectives: 22.9 us -> 0 us
  starting transfers between devices: 49 us -> 60.8 us
  waiting for transfers between devices: 3.09 us -> 14.2 us
  Pallas kernels: 0 us -> 5.66 us
  matrix products: 3.99 us -> 0 us
  local copies, waits for them, and re-layouts: 3.07 us -> 0.79 us
    all_gather x1 -> x0, blocking collectives: 22.9 us -> none  [on_device(): gradient = lax.all_gather(rows, FSDP, axis=0, tiled=True)]
    all_to_all x1 -> x2, waiting for transfers between devices: 0.01 us -> 9.27 us  [the longest x1 9.27 us: on_device(): lax.all_to_all(jnp.broadcast_to(rows[None], (8, 32, 512)), 'y', 0, 0, til...]
    all_to_all x1 -> x2, starting transfers between devices: 6.79 us -> 13.6 us  [the longest x1 6.82 us: on_device(): lax.all_to_all(jnp.broadcast_to(rows[None], (8, 32, 512)), 'y', 0, 0, til...]
    pallas_call x0 -> x2, Pallas kernels: none -> 5.66 us  [the longest x1 3.32 us: finish(): pl.pallas_call(finish_kernel, out_shape=(square, square, jax.ShapeDtypeSt...]
    ppermute x6, starting transfers between devices: 27 us -> 31.9 us  [rotate(): lax.ppermute(value, axis, [(i, (i + step) % size) for i in range(size)])]
    dot_general x3 -> x0, matrix products: 3.99 us -> none  [the longest x1 1.45 us: on_device(): product = jnp.dot(middle, right, preferred_element_type=jnp.float32)]
    another operation x1 -> x0, local copies, waits for them, and re-layouts: 2.76 us -> none  [on_device(): parts = grad_parts[0].reshape(6, 8, 32, 512)]
    ppermute x6, waiting for transfers between devices: 0.51 us -> 2.15 us  [rotate(): lax.ppermute(value, axis, [(i, (i + step) % size) for i in range(size)])]
  transfers between devices with their start and end apart: 8 -> 9, of which waited for: 2 -> 5; matrix products, arithmetic and copies ran while one was open for 4% -> 3% of each run, Pallas kernels for 0% -> 0%
where the time goes in v2:
time: 84.9 us; the launch traced here: 84.3 us
  starting transfers between devices  60.8 us (72%)
  waiting for transfers between devices  14.2 us (17%)
  Pallas kernels  5.66 us (7%)
  between operations  1.46 us (2%)
  other arithmetic  1.44 us (2%)
    ppermute x6, starting transfers between devices, rotate(): lax.ppermute(value, axis, [(i, (i + step) % size) for i in range(size)])  31.9 us
    all_to_all x1, starting transfers between devices, on_device(): parts = lax.all_to_all(parts, 'zh', 0, 0, tiled=True)  15.2 us
    all_to_all x1, waiting for transfers between devices, on_device(): lax.all_to_all(jnp.broadcast_to(rows[None], (8, 32, 512)), 'y', 0, 0, til...  9.27 us
    all_to_all x1, starting transfers between devices, on_device(): lax.all_to_all(jnp.broadcast_to(rows[None], (8, 32, 512)), 'y', 0, 0, til...  6.82 us
    all_to_all x1, starting transfers between devices, on_device(): parts = lax.all_to_all(parts, ('zl', 'x'), 0, 0, tiled=True)  6.8 us
    pallas_call x1, Pallas kernels, finish(): pl.pallas_call(finish_kernel, out_shape=(square, square, jax.ShapeDtypeSt...  3.32 us
    all_to_all x1, waiting for transfers between devices, on_device(): parts = lax.all_to_all(parts, 'zh', 0, 0, tiled=True)  2.74 us
    pallas_call x1, Pallas kernels, regroup(): pl.pallas_call(regroup_kernel, out_shape=jax.ShapeDtypeStruct((8, 6, 32,...  2.34 us
  transfers between devices with their start and end apart: 9, of which 5 were waited for; matrix products, arithmetic and copies ran while one was open for 3% of the time, Pallas kernels for 0%

profile of v2, /device:TPU:1, one launch (start us, length us, event | category | flops | bytes accessed | tf_op | source)
XLA Modules:
  0.0 84.3 jit_solution(3438466866139673348)
XLA Ops:
  0.6 2.3 %shard_map.85 = bf16[8,6,32,512]{3,2,1,0:T(8,128)(2,1)} custom-call(bf16[6,8,32,512]{3,2,1,0:T(8,128)(2,1)} %bitcast.23), custom_call_target="tpu_custom_call" | custom-call | tf_op jit(solution)/shard_map/pallas_call | solution.py:50
  3.0 0.0 copy-start.2
  3.0 0.0 copy-start.3
  3.0 6.8 %all-to-all-start = ((bf16[8,6,32,512]{3,2,1,0:T(8,128)(2,1)}), bf16[8,6,32,512]{3,2,1,0:T(8,128)(2,1)S(1)}, u32[]{:S(2)}, u32[]{:S(2)}) async-start(bf16[8,6,32,512]{3,2,1,0:T(8,128)(2,1)} %shard_map.85), calls=%async_computation | async-start | bytes 3145728 | tf_op jit(solution)/shard_map/all_to_all | solution.py:149
  9.8 0.0 copy-done.2
  9.8 0.1 fusion
  10.0 0.1 broadcast_select_fusion
  10.1 9.4 %collective-permute-start = (bf16[272,512]{1,0:T(8,128)(2,1)S(1)}, bf16[272,512]{1,0:T(8,128)(2,1)S(1)}, u32[]{:S(2)}, u32[]{:S(2)}) collective-permute-start(bf16[272,512]{1,0:T(8,128)(2,1)S(1)} %broadcast_select_fusion), channel_id=1, source_target_pairs={{0,1},{1,0},{2,3},{3,2},{4,5},{5,4},{6,7},{7,6},{8,9},{9,8},{10,11... | collective-permute-start | bytes 835592 | tf_op jit(solution)/shard_map/ppermute | solution.py:16
  20.1 0.5 collective-permute-done
  20.6 0.1 select_select_fusion.2
  20.7 1.9 %collective-permute-start.1 = (bf16[272,512]{1,0:T(8,128)(2,1)S(1)}, bf16[272,512]{1,0:T(8,128)(2,1)S(1)}, u32[]{:S(2)}, u32[]{:S(2)}) collective-permute-start(bf16[272,512]{1,0:T(8,128)(2,1)S(1)} %select_select_fusion.2), channel_id=1, source_target_pairs={{0,6},{2,8},{4,10},{6,12},{8,14},{10,0},{12,2},{14,4},{1,7},{3,9},... | collective-permute-start | bytes 835592 | tf_op jit(solution)/shard_map/ppermute | solution.py:16
  22.6 6.4 %collective-permute-start.2 = (bf16[272,512]{1,0:T(8,128)(2,1)S(1)}, bf16[272,512]{1,0:T(8,128)(2,1)S(1)}, u32[]{:S(2)}, u32[]{:S(2)}) collective-permute-start(bf16[272,512]{1,0:T(8,128)(2,1)S(1)} %select_select_fusion.2), channel_id=1, source_target_pairs={{0,10},{2,12},{4,14},{6,0},{8,2},{10,4},{12,6},{14,8},{1,11},{3,13... | collective-permute-start | bytes 835592 | tf_op jit(solution)/shard_map/ppermute | solution.py:16
  29.0 0.0 all-to-all-done
  29.0 0.9 %reduce_sum.36 = bf16[6,32,512]{2,1,0:T(8,128)(2,1)} reduce(bf16[8,6,32,512]{3,2,1,0:T(8,128)(2,1)S(1)} %all-to-all-done, bf16[]{:T(256)} %constant.34.clone.1), dimensions={0}, to_apply=%region_0.1 | reduce | flops 688128 | bytes 1769474 | tf_op jit(solution)/shard_map/reduce_sum | solution.py:150
  30.0 15.2 %all-to-all-start.1 = ((bf16[6,32,512]{2,1,0:T(8,128)(2,1)}), bf16[6,32,512]{2,1,0:T(8,128)(2,1)S(1)}, u32[]{:S(2)}, u32[]{:S(2)}) async-start(bf16[6,32,512]{2,1,0:T(8,128)(2,1)} %reduce_sum.36), calls=%async_computation.1 | async-start | bytes 393216 | tf_op jit(solution)/shard_map/all_to_all | solution.py:155
  45.2 0.0 collective-permute-done.1
  45.2 0.2 collective-permute-done.2
  45.4 3.0 %collective-permute-start.3 = (bf16[272,512]{1,0:T(8,128)(2,1)S(1)}, bf16[272,512]{1,0:T(8,128)(2,1)S(1)}, u32[]{:S(2)}, u32[]{:S(2)}) collective-permute-start(bf16[272,512]{1,0:T(8,128)(2,1)S(1)} %select_select_fusion.1), channel_id=1, source_target_pairs={{0,2},{2,4},{4,6},{6,8},{8,10},{10,12},{12,14},{14,0},{1,3},{3,5},... | collective-permute-start | bytes 835592 | tf_op jit(solution)/shard_map/ppermute | solution.py:16
  48.5 3.8 %collective-permute-start.4 = (bf16[272,512]{1,0:T(8,128)(2,1)S(1)}, bf16[272,512]{1,0:T(8,128)(2,1)S(1)}, u32[]{:S(2)}, u32[]{:S(2)}) collective-permute-start(bf16[272,512]{1,0:T(8,128)(2,1)S(1)} %select_select_fusion.1), channel_id=1, source_target_pairs={{0,14},{2,0},{4,2},{6,4},{8,6},{10,8},{12,10},{14,12},{1,15},{3,1}... | collective-permute-start | bytes 835592 | tf_op jit(solution)/shard_map/ppermute | solution.py:16
  52.3 2.7 %all-to-all-done.1 = bf16[6,32,512]{2,1,0:T(8,128)(2,1)S(1)} async-done(((bf16[6,32,512]{2,1,0:T(8,128)(2,1)}), bf16[6,32,512]{2,1,0:T(8,128)(2,1)S(1)}, u32[]{:S(2)}, u32[]{:S(2)}) %all-to-all-start.1) | async-done | bytes 196640 | tf_op jit(solution)/shard_map/all_to_all | solution.py:155
  55.1 0.0 copy-start
  55.1 0.0 copy-start.1
  55.1 0.7 broadcast_in_dim.25
  55.8 6.8 %all-to-all-start.2 = ((bf16[8,32,512]{2,1,0:T(8,128)(2,1)}), bf16[8,32,512]{2,1,0:T(8,128)(2,1)S(1)}, u32[]{:S(2)}, u32[]{:S(2)}) async-start(bf16[8,32,512]{2,1,0:T(8,128)(2,1)} %broadcast_in_dim.25), calls=%async_computation.2 | async-start | bytes 524288 | tf_op jit(solution)/shard_map/all_to_all | solution.py:158
  62.6 0.0 collective-permute-done.3
  62.7 0.0 collective-permute-done.4
  62.7 9.3 %all-to-all-done.2 = bf16[8,32,512]{2,1,0:T(8,128)(2,1)S(1)} async-done(((bf16[8,32,512]{2,1,0:T(8,128)(2,1)}), bf16[8,32,512]{2,1,0:T(8,128)(2,1)S(1)}, u32[]{:S(2)}, u32[]{:S(2)}) %all-to-all-start.2) | async-done | bytes 262176 | tf_op jit(solution)/shard_map/all_to_all | solution.py:158
  72.0 7.4 %collective-permute-start.5 = (bf16[528,512]{1,0:T(8,128)(2,1)S(1)}, bf16[528,512]{1,0:T(8,128)(2,1)S(1)}, u32[]{:S(2)}, u32[]{:S(2)}) collective-permute-start(bf16[528,512]{1,0:T(8,128)(2,1)S(1)} %pad_maximum_fusion.half), channel_id=1, source_target_pairs={{0,1},{1,0},{2,3},{3,2},{4,5},{5,4},{6,7},{7,6},{8,9},{9,8},{10,11... | collective-permute-start | bytes 1622024 | tf_op jit(solution)/shard_map/ppermute | solution.py:16
  79.5 0.1 pad_add_fusion.place
  79.5 1.5 %collective-permute-done.5.other = bf16[528,512]{1,0:T(8,128)(2,1)S(1)} collective-permute-done((bf16[528,512]{1,0:T(8,128)(2,1)S(1)}, bf16[528,512]{1,0:T(8,128)(2,1)S(1)}, u32[]{:S(2)}, u32[]{:S(2)}) %collective-permute-start.5) | collective-permute-done | bytes 540704 | tf_op jit(solution)/shard_map/ppermute | solution.py:16
  81.0 0.0 copy-done.1
  81.0 3.3 %shard_map.86 = (bf16[512,512]{1,0:T(8,128)(2,1)}, bf16[512,512]{1,0:T(8,128)(2,1)}, bf16[32,512]{1,0:T(8,128)(2,1)}) custom-call(s32[3]{0:T(128)S(1)} %pad_add_fusion.place, bf16[528,512]{1,0:T(8,128)(2,1)S(1)} %pad_maximum_fusion.half, bf16[528,512]{1,0:T(8,128)(2,1)S(1)} %collective-permute-done.5.other, bf16[512,512]{1,0:T(8,128)(2,1)S(1)} %bitcast.21, ...), custom_call_target="tpu_custom_call" | custom-call | flops 1073741824 | bytes 2097152 | tf_op jit(solution)/shard_map/pallas_call | solution.py:115
  (8 shorter events, 0.2 us)
Async XLA Ops:
  3.0 6.8 %copy-start.2 = (bf16[1,1,512,512]{3,2,1,0:T(8,128)(2,1)S(1)}, bf16[1,1,512,512]{3,2,1,0:T(8,128)(2,1)}, u32[]{:S(2)}) copy-start(bf16[1,1,512,512]{3,2,1,0:T(8,128)(2,1)} %param.11) | copy-start | bytes 1572868
  3.0 6.8 %copy-start.3 = (bf16[1,1,512,512]{3,2,1,0:T(8,128)(2,1)S(1)}, bf16[1,1,512,512]{3,2,1,0:T(8,128)(2,1)}, u32[]{:S(2)}) copy-start(bf16[1,1,512,512]{3,2,1,0:T(8,128)(2,1)} %param.10) | copy-start | bytes 1572868
  3.0 26.0 %all-to-all-start = ((bf16[8,6,32,512]{3,2,1,0:T(8,128)(2,1)}), bf16[8,6,32,512]{3,2,1,0:T(8,128)(2,1)S(1)}, u32[]{:S(2)}, u32[]{:S(2)}) async-start(bf16[8,6,32,512]{3,2,1,0:T(8,128)(2,1)} %shard_map.85), calls=%async_computation | async-start | bytes 3145728 | tf_op jit(solution)/shard_map/all_to_all | solution.py:149
  10.1 10.5 %collective-permute-start = (bf16[272,512]{1,0:T(8,128)(2,1)S(1)}, bf16[272,512]{1,0:T(8,128)(2,1)S(1)}, u32[]{:S(2)}, u32[]{:S(2)}) collective-permute-start(bf16[272,512]{1,0:T(8,128)(2,1)S(1)} %broadcast_select_fusion), channel_id=1, source_target_pairs={{0,1},{1,0},{2,3},{3,2},{4,5},{5,4},{6,7},{7,6},{8,9},{9,8},{10,11... | collective-permute-start | bytes 835592 | tf_op jit(solution)/shard_map/ppermute | solution.py:16
  20.7 24.5 %collective-permute-start.1 = (bf16[272,512]{1,0:T(8,128)(2,1)S(1)}, bf16[272,512]{1,0:T(8,128)(2,1)S(1)}, u32[]{:S(2)}, u32[]{:S(2)}) collective-permute-start(bf16[272,512]{1,0:T(8,128)(2,1)S(1)} %select_select_fusion.2), channel_id=1, source_target_pairs={{0,6},{2,8},{4,10},{6,12},{8,14},{10,0},{12,2},{14,4},{1,7},{3,9},... | collective-permute-start | bytes 835592 | tf_op jit(solution)/shard_map/ppermute | solution.py:16
  22.6 22.8 %collective-permute-start.2 = (bf16[272,512]{1,0:T(8,128)(2,1)S(1)}, bf16[272,512]{1,0:T(8,128)(2,1)S(1)}, u32[]{:S(2)}, u32[]{:S(2)}) collective-permute-start(bf16[272,512]{1,0:T(8,128)(2,1)S(1)} %select_select_fusion.2), channel_id=1, source_target_pairs={{0,10},{2,12},{4,14},{6,0},{8,2},{10,4},{12,6},{14,8},{1,11},{3,13... | collective-permute-start | bytes 835592 | tf_op jit(solution)/shard_map/ppermute | solution.py:16
  30.0 25.1 %all-to-all-start.1 = ((bf16[6,32,512]{2,1,0:T(8,128)(2,1)}), bf16[6,32,512]{2,1,0:T(8,128)(2,1)S(1)}, u32[]{:S(2)}, u32[]{:S(2)}) async-start(bf16[6,32,512]{2,1,0:T(8,128)(2,1)} %reduce_sum.36), calls=%async_computation.1 | async-start | bytes 393216 | tf_op jit(solution)/shard_map/all_to_all | solution.py:155
  45.4 17.2 %collective-permute-start.3 = (bf16[272,512]{1,0:T(8,128)(2,1)S(1)}, bf16[272,512]{1,0:T(8,128)(2,1)S(1)}, u32[]{:S(2)}, u32[]{:S(2)}) collective-permute-start(bf16[272,512]{1,0:T(8,128)(2,1)S(1)} %select_select_fusion.1), channel_id=1, source_target_pairs={{0,2},{2,4},{4,6},{6,8},{8,10},{10,12},{12,14},{14,0},{1,3},{3,5},... | collective-permute-start | bytes 835592 | tf_op jit(solution)/shard_map/ppermute | solution.py:16
  48.5 14.2 %collective-permute-start.4 = (bf16[272,512]{1,0:T(8,128)(2,1)S(1)}, bf16[272,512]{1,0:T(8,128)(2,1)S(1)}, u32[]{:S(2)}, u32[]{:S(2)}) collective-permute-start(bf16[272,512]{1,0:T(8,128)(2,1)S(1)} %select_select_fusion.1), channel_id=1, source_target_pairs={{0,14},{2,0},{4,2},{6,4},{8,6},{10,8},{12,10},{14,12},{1,15},{3,1}... | collective-permute-start | bytes 835592 | tf_op jit(solution)/shard_map/ppermute | solution.py:16
  55.1 25.9 %copy-start = (bf16[1,1,512,512]{3,2,1,0:T(8,128)(2,1)S(1)}, bf16[1,1,512,512]{3,2,1,0:T(8,128)(2,1)}, u32[]{:S(2)}) copy-start(bf16[1,1,512,512]{3,2,1,0:T(8,128)(2,1)} %param.8) | copy-start | bytes 1572868
  55.1 25.9 %copy-start.1 = (bf16[1,1,512,512]{3,2,1,0:T(8,128)(2,1)S(1)}, bf16[1,1,512,512]{3,2,1,0:T(8,128)(2,1)}, u32[]{:S(2)}) copy-start(bf16[1,1,512,512]{3,2,1,0:T(8,128)(2,1)} %param.9) | copy-start | bytes 1572868
  55.8 16.2 %all-to-all-start.2 = ((bf16[8,32,512]{2,1,0:T(8,128)(2,1)}), bf16[8,32,512]{2,1,0:T(8,128)(2,1)S(1)}, u32[]{:S(2)}, u32[]{:S(2)}) async-start(bf16[8,32,512]{2,1,0:T(8,128)(2,1)} %broadcast_in_dim.25), calls=%async_computation.2 | async-start | bytes 524288 | tf_op jit(solution)/shard_map/all_to_all | solution.py:158
  72.0 9.0 %collective-permute-start.5 = (bf16[528,512]{1,0:T(8,128)(2,1)S(1)}, bf16[528,512]{1,0:T(8,128)(2,1)S(1)}, u32[]{:S(2)}, u32[]{:S(2)}) collective-permute-start(bf16[528,512]{1,0:T(8,128)(2,1)S(1)} %pad_maximum_fusion.half), channel_id=1, source_target_pairs={{0,1},{1,0},{2,3},{3,2},{4,5},{5,4},{6,7},{7,6},{8,9},{9,8},{10,11... | collective-permute-start | bytes 1622024 | tf_op jit(solution)/shard_map/ppermute | solution.py:16

commit v3 on v2

--- a/solution.py
+++ b/solution.py
@@ -78,18 +78,6 @@
             gradient[pl.ds(at, 32), :] = source[y * 32 : y * 32 + 32, :]
         roots[pl.ds(pl.multiple_of(core * 256, 256), 256), :] = source[256:512, :]
     value = gradient[...]
-    owned = place[0] == 1
-    for slot, side, arrive, leave in ((left_slot, 1, into[0], out[0]), (right_slot, 0, into[1], out[1])):
-        gram = lax.dot_general(
-            value, value, (((side,), (side,)), ((), ())), preferred_element_type=jnp.float32
-        )
-        arrive.wait()
-
-        @pl.when(owned)
-        def add():
-            slot[...] = (slot[...].astype(jnp.float32) + gram).astype(jnp.bfloat16)
-
-        leave.start()
     both = roots[...]
     diagonal = half[512:528, :].astype(jnp.float32)[0:1, :]
     flipped = both.T.astype(jnp.float32)
@@ -99,6 +87,18 @@
     left = jnp.where(row <= col, both, flipped).astype(jnp.bfloat16)
     right = jnp.where(row > col, both, jnp.where(row < col, flipped, diagonal)).astype(jnp.bfloat16)
     middle = jnp.dot(left, value, preferred_element_type=jnp.float32).astype(jnp.bfloat16)
+    for slot, side, arrive, leave in ((left_slot, 1, into[0], out[0]), (right_slot, 0, into[1], out[1])):
+        arrive.wait()
+
+        @pl.when(place[0] == 1)
+        def add():
+            gram = lax.dot_general(
+                gradient[...], gradient[...], (((side,), (side,)), ((), ())),
+                preferred_element_type=jnp.float32,
+            )
+            slot[...] = (slot[...].astype(jnp.float32) + gram).astype(jnp.bfloat16)
+
+        leave.start()
     product[...] = jnp.dot(middle, right, preferred_element_type=jnp.float32)
     total = product[...]
     scale = lax.rsqrt(jnp.sum(total * total, keepdims=True) / (512.0 * 512.0) + epsilon)
@@ -143,7 +143,7 @@
     got = rotate(jnp.where(first, lower, upper), "core", 2, 1)
     here = jnp.where(holder == my_index, keep, got)
     up = rotate(here, "y", 8, 3)
-    down = rotate(here, "y", 8, -3)
+    down = rotate(here, "y", 8, -2)
 
     parts = regroup(grad_parts[0].reshape(6, 8, 32, 512))
     parts = lax.all_to_all(parts, ("zl", "x"), 0, 0, tiled=True)
@@ -155,9 +155,11 @@
     parts = lax.all_to_all(parts, "zh", 0, 0, tiled=True)
     rows = jnp.sum(parts.astype(jnp.float32), axis=0).astype(jnp.bfloat16)
 
+    up, down = after((up, down), parts)
+    kept = (away == 0) | (away == 3) | (away == 6)
+    here = jnp.where(kept, here, jnp.where((away == 2) | (away == 5), down, up))
+    rows, here = lax.optimization_barrier((rows, here))
     spread = lax.all_to_all(jnp.broadcast_to(rows[None], (8, 32, 512)), "y", 0, 0, tiled=True)
-    kept = (away == 0) | (away == 3) | (away == 5)
-    here = jnp.where(kept, here, jnp.where((away == 1) | (away == 4) | (away == 6), up, down))
     half = jnp.concatenate([spread.reshape(256, 512), here], axis=0)
     other = rotate(half, "core", 2, 1)
     left_out, right_out, update = finish(place, half, other, left_stat[0, 0], right_stat[0, 0])

time: 84.9 us -> 83.9 us (0.988)
  blocking collectives: 0 us -> 16.2 us
  starting transfers between devices: 60.8 us -> 51.9 us
  waiting for transfers between devices: 14.2 us -> 7.15 us
    all_to_all x0 -> x1, blocking collectives: none -> 16.2 us  [on_device(): lax.all_to_all(jnp.broadcast_to(rows[None], (8, 32, 512)), 'y', 0, 0, til...]
    all_to_all x1 -> x0, waiting for transfers between devices: 9.27 us -> none  [on_device(): lax.all_to_all(jnp.broadcast_to(rows[None], (8, 32, 512)), 'y', 0, 0, til...]
    all_to_all x1 -> x0, starting transfers between devices: 6.82 us -> none  [on_device(): lax.all_to_all(jnp.broadcast_to(rows[None], (8, 32, 512)), 'y', 0, 0, til...]
    ppermute x6, starting transfers between devices: 31.9 us -> 25.8 us  [rotate(): lax.ppermute(value, axis, [(i, (i + step) % size) for i in range(size)])]
    ppermute x6, waiting for transfers between devices: 2.15 us -> 6.74 us  [rotate(): lax.ppermute(value, axis, [(i, (i + step) % size) for i in range(size)])]
    all_to_all x1, starting transfers between devices: 15.2 us -> 19.3 us  [on_device(): parts = lax.all_to_all(parts, 'zh', 0, 0, tiled=True)]
    all_to_all x1, waiting for transfers between devices: 2.74 us -> 0.01 us  [on_device(): parts = lax.all_to_all(parts, 'zh', 0, 0, tiled=True)]
  transfers between devices with their start and end apart: 9 -> 8, of which waited for: 5 -> 5; matrix products, arithmetic and copies ran while one was open for 3% -> 2% of each run, Pallas kernels for 0% -> 0%
where the time goes in v3:
time: 83.9 us; the launch traced here: 83.4 us
  starting transfers between devices  51.9 us (62%)
  blocking collectives  16.2 us (19%)
  waiting for transfers between devices  7.15 us (9%)
  Pallas kernels  5.08 us (6%)
  between operations  1.52 us (2%)
  other arithmetic  1.45 us (2%)
    ppermute x6, starting transfers between devices, rotate(): lax.ppermute(value, axis, [(i, (i + step) % size) for i in range(size)])  25.8 us
    all_to_all x1, starting transfers between devices, on_device(): parts = lax.all_to_all(parts, 'zh', 0, 0, tiled=True)  19.3 us
    all_to_all x1, blocking collectives, on_device(): lax.all_to_all(jnp.broadcast_to(rows[None], (8, 32, 512)), 'y', 0, 0, til...  16.2 us
    all_to_all x1, starting transfers between devices, on_device(): parts = lax.all_to_all(parts, ('zl', 'x'), 0, 0, tiled=True)  6.8 us
    ppermute x6, waiting for transfers between devices, rotate(): lax.ppermute(value, axis, [(i, (i + step) % size) for i in range(size)])  6.74 us
    pallas_call x1, Pallas kernels, finish(): pl.pallas_call(finish_kernel, out_shape=(square, square, jax.ShapeDtypeSt...  2.76 us
    pallas_call x1, Pallas kernels, regroup(): pl.pallas_call(regroup_kernel, out_shape=jax.ShapeDtypeStruct((8, 6, 32,...  2.32 us
  transfers between devices with their start and end apart: 8, of which 5 were waited for; matrix products, arithmetic and copies ran while one was open for 2% of the time, Pallas kernels for 0%

profile of v3, /device:TPU:1, one launch (start us, length us, event | category | flops | bytes accessed | tf_op | source)
XLA Modules:
  0.0 83.4 jit_solution(17915894714142664432)
XLA Ops:
  0.6 2.3 %shard_map.85 = bf16[8,6,32,512]{3,2,1,0:T(8,128)(2,1)} custom-call(bf16[6,8,32,512]{3,2,1,0:T(8,128)(2,1)} %bitcast.23), custom_call_target="tpu_custom_call" | custom-call | tf_op jit(solution)/shard_map/pallas_call | solution.py:50
  3.0 0.0 copy-start.2
  3.0 0.0 copy-start.3
  3.0 6.8 %all-to-all-start = ((bf16[8,6,32,512]{3,2,1,0:T(8,128)(2,1)}), bf16[8,6,32,512]{3,2,1,0:T(8,128)(2,1)S(1)}, u32[]{:S(2)}, u32[]{:S(2)}) async-start(bf16[8,6,32,512]{3,2,1,0:T(8,128)(2,1)} %shard_map.85), calls=%async_computation | async-start | bytes 3145728 | tf_op jit(solution)/shard_map/all_to_all | solution.py:149
  9.8 0.0 copy-done.2
  9.8 0.0 copy-done.3
  9.8 0.1 fusion
  10.0 0.1 broadcast_select_fusion
  10.0 9.4 %collective-permute-start = (bf16[272,512]{1,0:T(8,128)(2,1)S(1)}, bf16[272,512]{1,0:T(8,128)(2,1)S(1)}, u32[]{:S(2)}, u32[]{:S(2)}) collective-permute-start(bf16[272,512]{1,0:T(8,128)(2,1)S(1)} %broadcast_select_fusion), channel_id=1, source_target_pairs={{0,1},{1,0},{2,3},{3,2},{4,5},{5,4},{6,7},{7,6},{8,9},{9,8},{10,11... | collective-permute-start | bytes 835592 | tf_op jit(solution)/shard_map/ppermute | solution.py:16
  20.1 0.5 collective-permute-done
  20.6 0.1 select_select_fusion.2
  20.7 1.9 %collective-permute-start.1 = (bf16[272,512]{1,0:T(8,128)(2,1)S(1)}, bf16[272,512]{1,0:T(8,128)(2,1)S(1)}, u32[]{:S(2)}, u32[]{:S(2)}) collective-permute-start(bf16[272,512]{1,0:T(8,128)(2,1)S(1)} %select_select_fusion.2), channel_id=1, source_target_pairs={{0,6},{2,8},{4,10},{6,12},{8,14},{10,0},{12,2},{14,4},{1,7},{3,9},... | collective-permute-start | bytes 835592 | tf_op jit(solution)/shard_map/ppermute | solution.py:16
  22.6 1.9 %collective-permute-start.2 = (bf16[272,512]{1,0:T(8,128)(2,1)S(1)}, bf16[272,512]{1,0:T(8,128)(2,1)S(1)}, u32[]{:S(2)}, u32[]{:S(2)}) collective-permute-start(bf16[272,512]{1,0:T(8,128)(2,1)S(1)} %select_select_fusion.2), channel_id=1, source_target_pairs={{0,12},{2,14},{4,0},{6,2},{8,4},{10,6},{12,8},{14,10},{1,13},{3,15... | collective-permute-start | bytes 835592 | tf_op jit(solution)/shard_map/ppermute | solution.py:16
  24.6 0.4 all-to-all-done
  25.0 0.9 %reduce_sum.36 = bf16[6,32,512]{2,1,0:T(8,128)(2,1)} reduce(bf16[8,6,32,512]{3,2,1,0:T(8,128)(2,1)S(1)} %all-to-all-done, bf16[]{:T(256)} %constant.32.clone.1), dimensions={0}, to_apply=%region_0.1 | reduce | flops 688128 | bytes 1769474 | tf_op jit(solution)/shard_map/reduce_sum | solution.py:150
  25.9 19.3 %all-to-all-start.1 = ((bf16[6,32,512]{2,1,0:T(8,128)(2,1)}), bf16[6,32,512]{2,1,0:T(8,128)(2,1)S(1)}, u32[]{:S(2)}, u32[]{:S(2)}) async-start(bf16[6,32,512]{2,1,0:T(8,128)(2,1)} %reduce_sum.36), calls=%async_computation.1 | async-start | bytes 393216 | tf_op jit(solution)/shard_map/all_to_all | solution.py:155
  45.2 0.0 collective-permute-done.1
  45.2 0.0 collective-permute-done.2
  45.2 3.2 %collective-permute-start.3 = (bf16[272,512]{1,0:T(8,128)(2,1)S(1)}, bf16[272,512]{1,0:T(8,128)(2,1)S(1)}, u32[]{:S(2)}, u32[]{:S(2)}) collective-permute-start(bf16[272,512]{1,0:T(8,128)(2,1)S(1)} %select_select_fusion.1), channel_id=1, source_target_pairs={{0,2},{2,4},{4,6},{6,8},{8,10},{10,12},{12,14},{14,0},{1,3},{3,5},... | collective-permute-start | bytes 835592 | tf_op jit(solution)/shard_map/ppermute | solution.py:16
  48.5 3.8 %collective-permute-start.4 = (bf16[272,512]{1,0:T(8,128)(2,1)S(1)}, bf16[272,512]{1,0:T(8,128)(2,1)S(1)}, u32[]{:S(2)}, u32[]{:S(2)}) collective-permute-start(bf16[272,512]{1,0:T(8,128)(2,1)S(1)} %select_select_fusion.1), channel_id=1, source_target_pairs={{0,14},{2,0},{4,2},{6,4},{8,6},{10,8},{12,10},{14,12},{1,15},{3,1}... | collective-permute-start | bytes 835592 | tf_op jit(solution)/shard_map/ppermute | solution.py:16
  52.3 0.0 copy-start
  52.3 0.0 copy-start.1
  52.3 3.9 %collective-permute-done.3 = bf16[272,512]{1,0:T(8,128)(2,1)S(1)} collective-permute-done((bf16[272,512]{1,0:T(8,128)(2,1)S(1)}, bf16[272,512]{1,0:T(8,128)(2,1)S(1)}, u32[]{:S(2)}, u32[]{:S(2)}) %collective-permute-start.3) | collective-permute-done | bytes 278560 | tf_op jit(solution)/shard_map/ppermute | solution.py:16
  56.2 0.9 %collective-permute-done.4 = bf16[272,512]{1,0:T(8,128)(2,1)S(1)} collective-permute-done((bf16[272,512]{1,0:T(8,128)(2,1)S(1)}, bf16[272,512]{1,0:T(8,128)(2,1)S(1)}, u32[]{:S(2)}, u32[]{:S(2)}) %collective-permute-start.4) | collective-permute-done | bytes 278560 | tf_op jit(solution)/shard_map/ppermute | solution.py:16
  57.1 0.0 all-to-all-done.1
  57.2 16.2 %all_to_all.15 = bf16[8,32,512]{2,1,0:T(8,128)(2,1)S(1)} all-to-all(bf16[8,32,512]{2,1,0:T(8,128)(2,1)S(1)} %broadcast_in_dim.27), channel_id=1, replica_groups=mesh['zh'=6,'zl'=2,'x'=4,'y'=8,'core'=2] {'y'}, dimensions={0} | all-to-all | bytes 524288 | tf_op jit(solution)/shard_map/all_to_all | solution.py:162
  73.5 5.6 %collective-permute-start.5 = (bf16[528,512]{1,0:T(8,128)(2,1)S(1)}, bf16[528,512]{1,0:T(8,128)(2,1)S(1)}, u32[]{:S(2)}, u32[]{:S(2)}) collective-permute-start(bf16[528,512]{1,0:T(8,128)(2,1)S(1)} %pad_maximum_fusion.half), channel_id=1, source_target_pairs={{0,1},{1,0},{2,3},{3,2},{4,5},{5,4},{6,7},{7,6},{8,9},{9,8},{10,11... | collective-permute-start | bytes 1622024 | tf_op jit(solution)/shard_map/ppermute | solution.py:16
  79.1 0.1 pad_add_fusion.place
  79.2 1.5 %collective-permute-done.5.other = bf16[528,512]{1,0:T(8,128)(2,1)S(1)} collective-permute-done((bf16[528,512]{1,0:T(8,128)(2,1)S(1)}, bf16[528,512]{1,0:T(8,128)(2,1)S(1)}, u32[]{:S(2)}, u32[]{:S(2)}) %collective-permute-start.5) | collective-permute-done | bytes 540704 | tf_op jit(solution)/shard_map/ppermute | solution.py:16
  80.6 0.0 copy-done
  80.6 0.0 copy-done.1
  80.6 2.8 %shard_map.86 = (bf16[512,512]{1,0:T(8,128)(2,1)}, bf16[512,512]{1,0:T(8,128)(2,1)}, bf16[32,512]{1,0:T(8,128)(2,1)}) custom-call(s32[3]{0:T(128)S(1)} %pad_add_fusion.place, bf16[528,512]{1,0:T(8,128)(2,1)S(1)} %pad_maximum_fusion.half, bf16[528,512]{1,0:T(8,128)(2,1)S(1)} %collective-permute-done.5.other, bf16[512,512]{1,0:T(8,128)(2,1)S(1)} %bitcast.21, ...), custom_call_target="tpu_custom_call" | custom-call | flops 1073741824 | bytes 2097152 | tf_op jit(solution)/shard_map/pallas_call | solution.py:115
  (7 shorter events, 0.2 us)
Async XLA Ops:
  3.0 6.8 %copy-start.2 = (bf16[1,1,512,512]{3,2,1,0:T(8,128)(2,1)S(1)}, bf16[1,1,512,512]{3,2,1,0:T(8,128)(2,1)}, u32[]{:S(2)}) copy-start(bf16[1,1,512,512]{3,2,1,0:T(8,128)(2,1)} %param.11) | copy-start | bytes 1572868
  3.0 6.8 %copy-start.3 = (bf16[1,1,512,512]{3,2,1,0:T(8,128)(2,1)S(1)}, bf16[1,1,512,512]{3,2,1,0:T(8,128)(2,1)}, u32[]{:S(2)}) copy-start(bf16[1,1,512,512]{3,2,1,0:T(8,128)(2,1)} %param.10) | copy-start | bytes 1572868
  3.0 22.0 %all-to-all-start = ((bf16[8,6,32,512]{3,2,1,0:T(8,128)(2,1)}), bf16[8,6,32,512]{3,2,1,0:T(8,128)(2,1)S(1)}, u32[]{:S(2)}, u32[]{:S(2)}) async-start(bf16[8,6,32,512]{3,2,1,0:T(8,128)(2,1)} %shard_map.85), calls=%async_computation | async-start | bytes 3145728 | tf_op jit(solution)/shard_map/all_to_all | solution.py:149
  10.0 10.5 %collective-permute-start = (bf16[272,512]{1,0:T(8,128)(2,1)S(1)}, bf16[272,512]{1,0:T(8,128)(2,1)S(1)}, u32[]{:S(2)}, u32[]{:S(2)}) collective-permute-start(bf16[272,512]{1,0:T(8,128)(2,1)S(1)} %broadcast_select_fusion), channel_id=1, source_target_pairs={{0,1},{1,0},{2,3},{3,2},{4,5},{5,4},{6,7},{7,6},{8,9},{9,8},{10,11... | collective-permute-start | bytes 835592 | tf_op jit(solution)/shard_map/ppermute | solution.py:16
  20.7 24.5 %collective-permute-start.1 = (bf16[272,512]{1,0:T(8,128)(2,1)S(1)}, bf16[272,512]{1,0:T(8,128)(2,1)S(1)}, u32[]{:S(2)}, u32[]{:S(2)}) collective-permute-start(bf16[272,512]{1,0:T(8,128)(2,1)S(1)} %select_select_fusion.2), channel_id=1, source_target_pairs={{0,6},{2,8},{4,10},{6,12},{8,14},{10,0},{12,2},{14,4},{1,7},{3,9},... | collective-permute-start | bytes 835592 | tf_op jit(solution)/shard_map/ppermute | solution.py:16
  22.6 22.6 %collective-permute-start.2 = (bf16[272,512]{1,0:T(8,128)(2,1)S(1)}, bf16[272,512]{1,0:T(8,128)(2,1)S(1)}, u32[]{:S(2)}, u32[]{:S(2)}) collective-permute-start(bf16[272,512]{1,0:T(8,128)(2,1)S(1)} %select_select_fusion.2), channel_id=1, source_target_pairs={{0,12},{2,14},{4,0},{6,2},{8,4},{10,6},{12,8},{14,10},{1,13},{3,15... | collective-permute-start | bytes 835592 | tf_op jit(solution)/shard_map/ppermute | solution.py:16
  25.9 31.2 %all-to-all-start.1 = ((bf16[6,32,512]{2,1,0:T(8,128)(2,1)}), bf16[6,32,512]{2,1,0:T(8,128)(2,1)S(1)}, u32[]{:S(2)}, u32[]{:S(2)}) async-start(bf16[6,32,512]{2,1,0:T(8,128)(2,1)} %reduce_sum.36), calls=%async_computation.1 | async-start | bytes 393216 | tf_op jit(solution)/shard_map/all_to_all | solution.py:155
  45.2 11.0 %collective-permute-start.3 = (bf16[272,512]{1,0:T(8,128)(2,1)S(1)}, bf16[272,512]{1,0:T(8,128)(2,1)S(1)}, u32[]{:S(2)}, u32[]{:S(2)}) collective-permute-start(bf16[272,512]{1,0:T(8,128)(2,1)S(1)} %select_select_fusion.1), channel_id=1, source_target_pairs={{0,2},{2,4},{4,6},{6,8},{8,10},{10,12},{12,14},{14,0},{1,3},{3,5},... | collective-permute-start | bytes 835592 | tf_op jit(solution)/shard_map/ppermute | solution.py:16
  48.5 8.6 %collective-permute-start.4 = (bf16[272,512]{1,0:T(8,128)(2,1)S(1)}, bf16[272,512]{1,0:T(8,128)(2,1)S(1)}, u32[]{:S(2)}, u32[]{:S(2)}) collective-permute-start(bf16[272,512]{1,0:T(8,128)(2,1)S(1)} %select_select_fusion.1), channel_id=1, source_target_pairs={{0,14},{2,0},{4,2},{6,4},{8,6},{10,8},{12,10},{14,12},{1,15},{3,1}... | collective-permute-start | bytes 835592 | tf_op jit(solution)/shard_map/ppermute | solution.py:16
  52.3 28.3 %copy-start = (bf16[1,1,512,512]{3,2,1,0:T(8,128)(2,1)S(1)}, bf16[1,1,512,512]{3,2,1,0:T(8,128)(2,1)}, u32[]{:S(2)}) copy-start(bf16[1,1,512,512]{3,2,1,0:T(8,128)(2,1)} %param.8) | copy-start | bytes 1572868
  52.3 28.3 %copy-start.1 = (bf16[1,1,512,512]{3,2,1,0:T(8,128)(2,1)S(1)}, bf16[1,1,512,512]{3,2,1,0:T(8,128)(2,1)}, u32[]{:S(2)}) copy-start(bf16[1,1,512,512]{3,2,1,0:T(8,128)(2,1)} %param.9) | copy-start | bytes 1572868
  73.5 7.1 %collective-permute-start.5 = (bf16[528,512]{1,0:T(8,128)(2,1)S(1)}, bf16[528,512]{1,0:T(8,128)(2,1)S(1)}, u32[]{:S(2)}, u32[]{:S(2)}) collective-permute-start(bf16[528,512]{1,0:T(8,128)(2,1)S(1)} %pad_maximum_fusion.half), channel_id=1, source_target_pairs={{0,1},{1,0},{2,3},{3,2},{4,5},{5,4},{6,7},{7,6},{8,9},{9,8},{10,11... | collective-permute-start | bytes 1622024 | tf_op jit(solution)/shard_map/ppermute | solution.py:16

commit v4 on v3

--- a/solution.py
+++ b/solution.py
@@ -32,15 +32,22 @@
 
 
 def regroup_kernel(source, target, held, sems):
-    into = [
-        pltpu.make_async_copy(source.at[:, to], held.at[to], sems.at[0, to]) for to in range(8)
-    ]
-    out = [pltpu.make_async_copy(held.at[to], target.at[to], sems.at[1, to]) for to in range(8)]
+    into, out = [], []
+    for to in range(8):
+        for part in range(2):
+            some = slice(3 * part, 3 * part + 3)
+            at = 2 * to + part
+            into.append(
+                pltpu.make_async_copy(source.at[some, to], held.at[to, some], sems.at[0, at])
+            )
+            out.append(
+                pltpu.make_async_copy(held.at[to, some], target.at[to, some], sems.at[1, at])
+            )
     for copy in into:
         copy.start()
-    for to in range(8):
-        into[to].wait()
-        out[to].start()
+    for arrive, leave in zip(into, out):
+        arrive.wait()
+        leave.start()
     for copy in out:
         copy.wait()
 
@@ -54,7 +61,7 @@
         out_specs=anywhere,
         scratch_shapes=[
             pltpu.VMEM((8, 6, 32, 512), jnp.bfloat16),
-            pltpu.SemaphoreType.DMA((2, 8)),
+            pltpu.SemaphoreType.DMA((2, 16)),
         ],
         compiler_params=pltpu.CompilerParams(vmem_limit_bytes=62 * 1024 * 1024),
     )(parts)

time: 83.9 us -> 84 us (level)
  no operation moved by 1% of the time
where the time goes in v4:
time: 84 us; the launch traced here: 83.5 us
  starting transfers between devices  51.9 us (62%)
  blocking collectives  16.2 us (19%)
  waiting for transfers between devices  7.15 us (9%)
  Pallas kernels  5.19 us (6%)
  between operations  1.52 us (2%)
  other arithmetic  1.45 us (2%)
    ppermute x6, starting transfers between devices, rotate(): lax.ppermute(value, axis, [(i, (i + step) % size) for i in range(size)])  25.8 us
    all_to_all x1, starting transfers between devices, on_device(): parts = lax.all_to_all(parts, 'zh', 0, 0, tiled=True)  19.3 us
    all_to_all x1, blocking collectives, on_device(): lax.all_to_all(jnp.broadcast_to(rows[None], (8, 32, 512)), 'y', 0, 0, til...  16.2 us
    all_to_all x1, starting transfers between devices, on_device(): parts = lax.all_to_all(parts, ('zl', 'x'), 0, 0, tiled=True)  6.8 us
    ppermute x6, waiting for transfers between devices, rotate(): lax.ppermute(value, axis, [(i, (i + step) % size) for i in range(size)])  6.74 us
    pallas_call x1, Pallas kernels, finish(): pl.pallas_call(finish_kernel, out_shape=(square, square, jax.ShapeDtypeSt...  2.76 us
    pallas_call x1, Pallas kernels, regroup(): pl.pallas_call(regroup_kernel, out_shape=jax.ShapeDtypeStruct((8, 6, 32,...  2.43 us
  transfers between devices with their start and end apart: 8, of which 5 were waited for; matrix products, arithmetic and copies ran while one was open for 2% of the time, Pallas kernels for 0%

profile of v4, /device:TPU:1, one launch (start us, length us, event | category | flops | bytes accessed | tf_op | source)
XLA Modules:
  0.0 83.5 jit_solution(18325931102139437618)
XLA Ops:
  0.6 2.4 %shard_map.85 = bf16[8,6,32,512]{3,2,1,0:T(8,128)(2,1)} custom-call(bf16[6,8,32,512]{3,2,1,0:T(8,128)(2,1)} %bitcast.23), custom_call_target="tpu_custom_call" | custom-call | tf_op jit(solution)/shard_map/pallas_call | solution.py:57
  3.1 0.0 copy-start.2
  3.1 0.0 copy-start.3
  3.1 6.8 %all-to-all-start = ((bf16[8,6,32,512]{3,2,1,0:T(8,128)(2,1)}), bf16[8,6,32,512]{3,2,1,0:T(8,128)(2,1)S(1)}, u32[]{:S(2)}, u32[]{:S(2)}) async-start(bf16[8,6,32,512]{3,2,1,0:T(8,128)(2,1)} %shard_map.85), calls=%async_computation | async-start | bytes 3145728 | tf_op jit(solution)/shard_map/all_to_all | solution.py:156
  9.9 0.0 copy-done.2
  9.9 0.0 copy-done.3
  9.9 0.1 fusion
  10.1 0.1 broadcast_select_fusion
  10.1 9.4 %collective-permute-start = (bf16[272,512]{1,0:T(8,128)(2,1)S(1)}, bf16[272,512]{1,0:T(8,128)(2,1)S(1)}, u32[]{:S(2)}, u32[]{:S(2)}) collective-permute-start(bf16[272,512]{1,0:T(8,128)(2,1)S(1)} %broadcast_select_fusion), channel_id=1, source_target_pairs={{0,1},{1,0},{2,3},{3,2},{4,5},{5,4},{6,7},{7,6},{8,9},{9,8},{10,11... | collective-permute-start | bytes 835592 | tf_op jit(solution)/shard_map/ppermute | solution.py:16
  20.2 0.5 collective-permute-done
  20.7 0.1 select_select_fusion.2
  20.8 1.9 %collective-permute-start.1 = (bf16[272,512]{1,0:T(8,128)(2,1)S(1)}, bf16[272,512]{1,0:T(8,128)(2,1)S(1)}, u32[]{:S(2)}, u32[]{:S(2)}) collective-permute-start(bf16[272,512]{1,0:T(8,128)(2,1)S(1)} %select_select_fusion.2), channel_id=1, source_target_pairs={{0,6},{2,8},{4,10},{6,12},{8,14},{10,0},{12,2},{14,4},{1,7},{3,9},... | collective-permute-start | bytes 835592 | tf_op jit(solution)/shard_map/ppermute | solution.py:16
  22.7 1.9 %collective-permute-start.2 = (bf16[272,512]{1,0:T(8,128)(2,1)S(1)}, bf16[272,512]{1,0:T(8,128)(2,1)S(1)}, u32[]{:S(2)}, u32[]{:S(2)}) collective-permute-start(bf16[272,512]{1,0:T(8,128)(2,1)S(1)} %select_select_fusion.2), channel_id=1, source_target_pairs={{0,12},{2,14},{4,0},{6,2},{8,4},{10,6},{12,8},{14,10},{1,13},{3,15... | collective-permute-start | bytes 835592 | tf_op jit(solution)/shard_map/ppermute | solution.py:16
  24.7 0.4 all-to-all-done
  25.1 0.9 %reduce_sum.36 = bf16[6,32,512]{2,1,0:T(8,128)(2,1)} reduce(bf16[8,6,32,512]{3,2,1,0:T(8,128)(2,1)S(1)} %all-to-all-done, bf16[]{:T(256)} %constant.32.clone.1), dimensions={0}, to_apply=%region_0.1 | reduce | flops 688128 | bytes 1769474 | tf_op jit(solution)/shard_map/reduce_sum | solution.py:157
  26.0 19.3 %all-to-all-start.1 = ((bf16[6,32,512]{2,1,0:T(8,128)(2,1)}), bf16[6,32,512]{2,1,0:T(8,128)(2,1)S(1)}, u32[]{:S(2)}, u32[]{:S(2)}) async-start(bf16[6,32,512]{2,1,0:T(8,128)(2,1)} %reduce_sum.36), calls=%async_computation.1 | async-start | bytes 393216 | tf_op jit(solution)/shard_map/all_to_all | solution.py:162
  45.3 0.0 collective-permute-done.1
  45.3 0.0 collective-permute-done.2
  45.4 3.2 %collective-permute-start.3 = (bf16[272,512]{1,0:T(8,128)(2,1)S(1)}, bf16[272,512]{1,0:T(8,128)(2,1)S(1)}, u32[]{:S(2)}, u32[]{:S(2)}) collective-permute-start(bf16[272,512]{1,0:T(8,128)(2,1)S(1)} %select_select_fusion.1), channel_id=1, source_target_pairs={{0,2},{2,4},{4,6},{6,8},{8,10},{10,12},{12,14},{14,0},{1,3},{3,5},... | collective-permute-start | bytes 835592 | tf_op jit(solution)/shard_map/ppermute | solution.py:16
  48.6 3.8 %collective-permute-start.4 = (bf16[272,512]{1,0:T(8,128)(2,1)S(1)}, bf16[272,512]{1,0:T(8,128)(2,1)S(1)}, u32[]{:S(2)}, u32[]{:S(2)}) collective-permute-start(bf16[272,512]{1,0:T(8,128)(2,1)S(1)} %select_select_fusion.1), channel_id=1, source_target_pairs={{0,14},{2,0},{4,2},{6,4},{8,6},{10,8},{12,10},{14,12},{1,15},{3,1}... | collective-permute-start | bytes 835592 | tf_op jit(solution)/shard_map/ppermute | solution.py:16
  52.4 0.0 copy-start
  52.4 0.0 copy-start.1
  52.4 3.9 %collective-permute-done.3 = bf16[272,512]{1,0:T(8,128)(2,1)S(1)} collective-permute-done((bf16[272,512]{1,0:T(8,128)(2,1)S(1)}, bf16[272,512]{1,0:T(8,128)(2,1)S(1)}, u32[]{:S(2)}, u32[]{:S(2)}) %collective-permute-start.3) | collective-permute-done | bytes 278560 | tf_op jit(solution)/shard_map/ppermute | solution.py:16
  56.3 0.9 %collective-permute-done.4 = bf16[272,512]{1,0:T(8,128)(2,1)S(1)} collective-permute-done((bf16[272,512]{1,0:T(8,128)(2,1)S(1)}, bf16[272,512]{1,0:T(8,128)(2,1)S(1)}, u32[]{:S(2)}, u32[]{:S(2)}) %collective-permute-start.4) | collective-permute-done | bytes 278560 | tf_op jit(solution)/shard_map/ppermute | solution.py:16
  57.2 0.0 all-to-all-done.1
  57.3 16.2 %all_to_all.15 = bf16[8,32,512]{2,1,0:T(8,128)(2,1)S(1)} all-to-all(bf16[8,32,512]{2,1,0:T(8,128)(2,1)S(1)} %broadcast_in_dim.27), channel_id=1, replica_groups=mesh['zh'=6,'zl'=2,'x'=4,'y'=8,'core'=2] {'y'}, dimensions={0} | all-to-all | bytes 524288 | tf_op jit(solution)/shard_map/all_to_all | solution.py:169
  73.6 5.6 %collective-permute-start.5 = (bf16[528,512]{1,0:T(8,128)(2,1)S(1)}, bf16[528,512]{1,0:T(8,128)(2,1)S(1)}, u32[]{:S(2)}, u32[]{:S(2)}) collective-permute-start(bf16[528,512]{1,0:T(8,128)(2,1)S(1)} %pad_maximum_fusion.half), channel_id=1, source_target_pairs={{0,1},{1,0},{2,3},{3,2},{4,5},{5,4},{6,7},{7,6},{8,9},{9,8},{10,11... | collective-permute-start | bytes 1622024 | tf_op jit(solution)/shard_map/ppermute | solution.py:16
  79.2 0.1 pad_add_fusion.place
  79.3 1.5 %collective-permute-done.5.other = bf16[528,512]{1,0:T(8,128)(2,1)S(1)} collective-permute-done((bf16[528,512]{1,0:T(8,128)(2,1)S(1)}, bf16[528,512]{1,0:T(8,128)(2,1)S(1)}, u32[]{:S(2)}, u32[]{:S(2)}) %collective-permute-start.5) | collective-permute-done | bytes 540704 | tf_op jit(solution)/shard_map/ppermute | solution.py:16
  80.7 0.0 copy-done
  80.7 0.0 copy-done.1
  80.7 2.8 %shard_map.86 = (bf16[512,512]{1,0:T(8,128)(2,1)}, bf16[512,512]{1,0:T(8,128)(2,1)}, bf16[32,512]{1,0:T(8,128)(2,1)}) custom-call(s32[3]{0:T(128)S(1)} %pad_add_fusion.place, bf16[528,512]{1,0:T(8,128)(2,1)S(1)} %pad_maximum_fusion.half, bf16[528,512]{1,0:T(8,128)(2,1)S(1)} %collective-permute-done.5.other, bf16[512,512]{1,0:T(8,128)(2,1)S(1)} %bitcast.21, ...), custom_call_target="tpu_custom_call" | custom-call | flops 1073741824 | bytes 2097152 | tf_op jit(solution)/shard_map/pallas_call | solution.py:122
  (7 shorter events, 0.2 us)
Async XLA Ops:
  3.1 6.8 %copy-start.2 = (bf16[1,1,512,512]{3,2,1,0:T(8,128)(2,1)S(1)}, bf16[1,1,512,512]{3,2,1,0:T(8,128)(2,1)}, u32[]{:S(2)}) copy-start(bf16[1,1,512,512]{3,2,1,0:T(8,128)(2,1)} %param.11) | copy-start | bytes 1572868
  3.1 6.8 %copy-start.3 = (bf16[1,1,512,512]{3,2,1,0:T(8,128)(2,1)S(1)}, bf16[1,1,512,512]{3,2,1,0:T(8,128)(2,1)}, u32[]{:S(2)}) copy-start(bf16[1,1,512,512]{3,2,1,0:T(8,128)(2,1)} %param.10) | copy-start | bytes 1572868
  3.1 22.0 %all-to-all-start = ((bf16[8,6,32,512]{3,2,1,0:T(8,128)(2,1)}), bf16[8,6,32,512]{3,2,1,0:T(8,128)(2,1)S(1)}, u32[]{:S(2)}, u32[]{:S(2)}) async-start(bf16[8,6,32,512]{3,2,1,0:T(8,128)(2,1)} %shard_map.85), calls=%async_computation | async-start | bytes 3145728 | tf_op jit(solution)/shard_map/all_to_all | solution.py:156
  10.1 10.5 %collective-permute-start = (bf16[272,512]{1,0:T(8,128)(2,1)S(1)}, bf16[272,512]{1,0:T(8,128)(2,1)S(1)}, u32[]{:S(2)}, u32[]{:S(2)}) collective-permute-start(bf16[272,512]{1,0:T(8,128)(2,1)S(1)} %broadcast_select_fusion), channel_id=1, source_target_pairs={{0,1},{1,0},{2,3},{3,2},{4,5},{5,4},{6,7},{7,6},{8,9},{9,8},{10,11... | collective-permute-start | bytes 835592 | tf_op jit(solution)/shard_map/ppermute | solution.py:16
  20.8 24.5 %collective-permute-start.1 = (bf16[272,512]{1,0:T(8,128)(2,1)S(1)}, bf16[272,512]{1,0:T(8,128)(2,1)S(1)}, u32[]{:S(2)}, u32[]{:S(2)}) collective-permute-start(bf16[272,512]{1,0:T(8,128)(2,1)S(1)} %select_select_fusion.2), channel_id=1, source_target_pairs={{0,6},{2,8},{4,10},{6,12},{8,14},{10,0},{12,2},{14,4},{1,7},{3,9},... | collective-permute-start | bytes 835592 | tf_op jit(solution)/shard_map/ppermute | solution.py:16
  22.7 22.6 %collective-permute-start.2 = (bf16[272,512]{1,0:T(8,128)(2,1)S(1)}, bf16[272,512]{1,0:T(8,128)(2,1)S(1)}, u32[]{:S(2)}, u32[]{:S(2)}) collective-permute-start(bf16[272,512]{1,0:T(8,128)(2,1)S(1)} %select_select_fusion.2), channel_id=1, source_target_pairs={{0,12},{2,14},{4,0},{6,2},{8,4},{10,6},{12,8},{14,10},{1,13},{3,15... | collective-permute-start | bytes 835592 | tf_op jit(solution)/shard_map/ppermute | solution.py:16
  26.0 31.2 %all-to-all-start.1 = ((bf16[6,32,512]{2,1,0:T(8,128)(2,1)}), bf16[6,32,512]{2,1,0:T(8,128)(2,1)S(1)}, u32[]{:S(2)}, u32[]{:S(2)}) async-start(bf16[6,32,512]{2,1,0:T(8,128)(2,1)} %reduce_sum.36), calls=%async_computation.1 | async-start | bytes 393216 | tf_op jit(solution)/shard_map/all_to_all | solution.py:162
  45.4 11.0 %collective-permute-start.3 = (bf16[272,512]{1,0:T(8,128)(2,1)S(1)}, bf16[272,512]{1,0:T(8,128)(2,1)S(1)}, u32[]{:S(2)}, u32[]{:S(2)}) collective-permute-start(bf16[272,512]{1,0:T(8,128)(2,1)S(1)} %select_select_fusion.1), channel_id=1, source_target_pairs={{0,2},{2,4},{4,6},{6,8},{8,10},{10,12},{12,14},{14,0},{1,3},{3,5},... | collective-permute-start | bytes 835592 | tf_op jit(solution)/shard_map/ppermute | solution.py:16
  48.6 8.6 %collective-permute-start.4 = (bf16[272,512]{1,0:T(8,128)(2,1)S(1)}, bf16[272,512]{1,0:T(8,128)(2,1)S(1)}, u32[]{:S(2)}, u32[]{:S(2)}) collective-permute-start(bf16[272,512]{1,0:T(8,128)(2,1)S(1)} %select_select_fusion.1), channel_id=1, source_target_pairs={{0,14},{2,0},{4,2},{6,4},{8,6},{10,8},{12,10},{14,12},{1,15},{3,1}... | collective-permute-start | bytes 835592 | tf_op jit(solution)/shard_map/ppermute | solution.py:16
  52.4 28.3 %copy-start = (bf16[1,1,512,512]{3,2,1,0:T(8,128)(2,1)S(1)}, bf16[1,1,512,512]{3,2,1,0:T(8,128)(2,1)}, u32[]{:S(2)}) copy-start(bf16[1,1,512,512]{3,2,1,0:T(8,128)(2,1)} %param.8) | copy-start | bytes 1572868
  52.4 28.3 %copy-start.1 = (bf16[1,1,512,512]{3,2,1,0:T(8,128)(2,1)S(1)}, bf16[1,1,512,512]{3,2,1,0:T(8,128)(2,1)}, u32[]{:S(2)}) copy-start(bf16[1,1,512,512]{3,2,1,0:T(8,128)(2,1)} %param.9) | copy-start | bytes 1572868
  73.6 7.1 %collective-permute-start.5 = (bf16[528,512]{1,0:T(8,128)(2,1)S(1)}, bf16[528,512]{1,0:T(8,128)(2,1)S(1)}, u32[]{:S(2)}, u32[]{:S(2)}) collective-permute-start(bf16[528,512]{1,0:T(8,128)(2,1)S(1)} %pad_maximum_fusion.half), channel_id=1, source_target_pairs={{0,1},{1,0},{2,3},{3,2},{4,5},{5,4},{6,7},{7,6},{8,9},{9,8},{10,11... | collective-permute-start | bytes 1622024 | tf_op jit(solution)/shard_map/ppermute | solution.py:16
